TPU v7x, 256 devices: a whole 4x4x8 slice. The times are simulated.
256 devices in a mesh: seq: 32 (over x, y, core), kvh: 8 (over z).
Axes of the slice: x: 4, y: 4, z: 8, core: 2. Of those that a mesh axis runs over, the one named last changes fastest.
Arguments:
- queries: bfloat16 [512, 64, 128], P(('seq', 'kvh')), may hold values from -9 to 9
- attn_out: bfloat16 [512, 64, 128], P(('seq', 'kvh')), may hold values from -0.59765625 to 0.59765625
- grad_out: bfloat16 [512, 64, 128], P(('seq', 'kvh')), may hold values from -384 to 384
- log_norms: float32 [512, 64], P(('seq', 'kvh')), may hold values from 0 to 14, as said below
- query_starts: int32 [512], replicated, may hold values from 0 to 8192
- keys: bfloat16 [32768, 8, 128], P('seq', 'kvh'), may hold values from -6 to 6
- values: bfloat16 [32768, 8, 128], P('seq', 'kvh'), may hold values from -6 to 6
Outputs:
- grad_query: bfloat16 [512, 64, 128], P(('seq', 'kvh'))
- grad_keys: bfloat16 [32768, 8, 128], P('seq', 'kvh')
- grad_values: bfloat16 [32768, 8, 128], P('seq', 'kvh')
Inputs may be any that keep to these rules, and one draw needn't show every extreme that they name: `log_norms`: each entry lies within one of the log of its token's number of visible positions plus 1.125.
All inputs are finite; a program needn't handle non-finite values.
Results may differ from a plain program's by a relative error of at most 0.0052.
Values may be sent and summed in bfloat16 or wider, within the bound.
A program may use at most 64 MiB of HBM per device.

v0:
```python
import math

import jax
import jax.numpy as jnp
from jax import lax
from jax.sharding import PartitionSpec as P


def in_one_piece(arrays, axis, split_dim, concat_dim, along):
    widths = [math.prod(a.shape[along:]) for a in arrays]
    both = jnp.concatenate(
        [a.reshape(*a.shape[:along], w) for a, w in zip(arrays, widths)], axis=along
    )
    result = lax.all_to_all(both, axis, split_axis=split_dim, concat_axis=concat_dim, tiled=True)
    blocks = jnp.split(result, [sum(widths[:k]) for k in range(1, len(widths))], axis=along)
    return tuple(
        (b.reshape(*result.shape[:along], *a.shape[along:]) for a, b in zip(arrays, blocks))
    )


def shifted(value, axis, by):
    peers = lax.axis_size(axis)
    return lax.ppermute(value, axis, [(i, (i + by) % peers) for i in range(peers)])


def local(queries, attn_out, grad_out, log_norms, query_starts, keys, values):
    scaling = queries.shape[-1] ** (-0.5)
    seq_count = lax.axis_size("seq")
    seq_index = lax.axis_index("seq")
    deltas = jnp.sum(grad_out.astype(jnp.float32) * attn_out.astype(jnp.float32), axis=-1)
    query_wide, grad_wide, norm_block, delta_block = in_one_piece(
        (queries.astype(jnp.float32), grad_out.astype(jnp.float32), log_norms, deltas),
        "kvh",
        1,
        0,
        2,
    )
    query_block = query_wide.astype(jnp.bfloat16)
    grad_block = grad_wide.astype(jnp.bfloat16)
    block_rows = query_block.shape[0]
    total_rows = block_rows * seq_count
    key_count = keys.shape[0]
    key_rows = keys[:, 0, :]
    value_rows = values[:, 0, :]
    key_pos = seq_index * key_count + jnp.arange(key_count, dtype=jnp.int32)
    offset = key_count * seq_count - total_rows

    def block_terms(queries_in, grads_in, norms_in, deltas_in, first_row):
        row_count = queries_in.shape[0]
        query_pos = offset + first_row + jnp.arange(row_count, dtype=jnp.int32)
        first_keys = lax.dynamic_slice_in_dim(query_starts, first_row, row_count)
        visible = (key_pos[None, :] >= first_keys[:, None]) & (
            key_pos[None, :] <= query_pos[:, None]
        )
        scores = (
            jnp.einsum("rgd,kd->rgk", queries_in, key_rows, preferred_element_type=jnp.float32)
            * scaling
        )
        weights = jnp.where(visible[:, None, :], jnp.exp(scores - norms_in[..., None]), 0.0)
        weight_grad = jnp.einsum(
            "rgd,kd->rgk", grads_in, value_rows, preferred_element_type=jnp.float32
        )
        score_grad = weights * (weight_grad - deltas_in[..., None])
        weight_half = weights.astype(jnp.bfloat16)
        score_half = score_grad.astype(jnp.bfloat16)
        value_part = jnp.einsum(
            "rgk,rgd->kd", weight_half, grads_in, preferred_element_type=jnp.float32
        )
        key_part = (
            jnp.einsum("rgk,rgd->kd", score_half, queries_in, preferred_element_type=jnp.float32)
            * scaling
        )
        query_part = (
            jnp.einsum("rgk,kd->rgd", score_half, key_rows, preferred_element_type=jnp.float32)
            * scaling
        )
        return (key_part, value_part, query_part)

    key_empty = jnp.zeros(key_rows.shape, jnp.float32)

    def visit_owner(counter, carried):
        query_now, grad_now, norm_now, delta_now, query_grad, key_grad, value_grad = carried
        anchor = (seq_index - counter) % seq_count
        key_part, value_part, query_part = block_terms(
            query_now, grad_now, norm_now, delta_now, anchor * block_rows
        )
        query_wide, grad_wide, norm_now, delta_now, query_grad = shifted(
            (
                query_now.astype(jnp.float32),
                grad_now.astype(jnp.float32),
                norm_now,
                delta_now,
                query_grad + query_part,
            ),
            "seq",
            1,
        )
        query_now = query_wide.astype(jnp.bfloat16)
        grad_now = grad_wide.astype(jnp.bfloat16)
        return (
            query_now,
            grad_now,
            norm_now,
            delta_now,
            query_grad,
            key_grad + key_part,
            value_grad + value_part,
        )

    query_empty = jnp.zeros(query_block.shape, jnp.float32)
    carried = (query_block, grad_block, norm_block, delta_block, query_empty, key_empty, key_empty)
    carried = lax.fori_loop(0, seq_count - 1, visit_owner, carried)
    query_now, grad_now, norm_now, delta_now, query_grad, key_grad, value_grad = carried
    anchor = (seq_index + 1) % seq_count
    key_part, value_part, query_part = block_terms(
        query_now, grad_now, norm_now, delta_now, anchor * block_rows
    )
    key_grad = key_grad + key_part
    value_grad = value_grad + value_part
    query_grad = shifted((query_grad + query_part).astype(jnp.bfloat16), "seq", 1).astype(
        jnp.float32
    )
    grad_query = lax.all_to_all(
        query_grad.astype(jnp.bfloat16), "kvh", split_axis=0, concat_axis=1, tiled=True
    )
    return (
        grad_query,
        key_grad.astype(jnp.bfloat16)[:, None, :],
        value_grad.astype(jnp.bfloat16)[:, None, :],
    )


def solution(mesh):
    return jax.shard_map(
        local,
        mesh=mesh,
        in_specs=(
            P(("seq", "kvh"), None, None),
            P(("seq", "kvh"), None, None),
            P(("seq", "kvh"), None, None),
            P(("seq", "kvh"), None),
            P(),
            P("seq", "kvh", None),
            P("seq", "kvh", None),
        ),
        out_specs=(P(("seq", "kvh"), None, None), P("seq", "kvh", None), P("seq", "kvh", None)),
        check_vma=False,
    )
```

profile of v0, /device:TPU:2, one launch (start us, length us, event | category | flops | bytes accessed | tf_op | source)
XLA Modules:
  0.0 316.0 jit_solution(12219225037534676147)
XLA Ops:
  4.2 8.5 %all-to-all-start = ((f32[2,64,258]{2,0,1:T(2,128)}), f32[2,64,258]{2,0,1:T(2,128)S(1)}, u32[]{:S(2)}, u32[]{:S(2)}) async-start(f32[2,64,258]{2,0,1:T(2,128)} %copy.80), calls=%async_computation | async-start | bytes 393216 | tf_op jit(solution)/shard_map/all_to_all | solution.py:14
  13.5 9.6 %all-to-all-done = f32[2,64,258]{2,0,1:T(2,128)S(1)} async-done(((f32[2,64,258]{2,0,1:T(2,128)}), f32[2,64,258]{2,0,1:T(2,128)S(1)}, u32[]{:S(2)}, u32[]{:S(2)}) %all-to-all-start) | async-done | bytes 132128 | tf_op jit(solution)/shard_map/all_to_all | solution.py:14
  24.2 273.5 %while.28 = (s32[]{:T(128)}, bf16[16,8,128]{2,1,0:T(8,128)(2,1)S(1)}, bf16[16,8,128]{2,1,0:T(8,128)(2,1)S(1)}, f32[16,8]{1,0:T(8,128)S(1)}, f32[16,8]{1,0:T(8,12...) while((s32[]{:T(128)}, ...), condition=%wide.region_2.3_spmd.clone, body=%wide.region_1.2_spmd.clone.sunk | while | flops 169428000 | bytes 6209415 | solution.py:112
  31.2 3.2 %collective-permute-done.4 = f32[16,8,128]{2,1,0:T(8,128)S(1)} collective-permute-done((f32[16,8,128]{2,1,0:T(8,128)S(1)}, f32[16,8,128]{2,1,0:T(8,128)S(1)}, u32[]{:S(2)}, u32[]{:S(2)}) %collective-permute-start.4) | collective-permute-done | bytes 65568 | tf_op jit(solution)/shard_map/while/body/eval_jaxpr/ppermute | solution.py:23
  36.7 3.5 %collective-permute-done.2 = f32[16,8]{1,0:T(8,128)S(1)} collective-permute-done((f32[16,8]{1,0:T(8,128)S(1)}, f32[16,8]{1,0:T(8,128)S(1)}, u32[]{:S(2)}, u32[]{:S(2)}) %collective-permute-start.2) | collective-permute-done | bytes 544 | tf_op jit(solution)/shard_map/while/body/eval_jaxpr/ppermute | solution.py:23
  48.0 4.0 %collective-permute-done.4 = f32[16,8,128]{2,1,0:T(8,128)S(1)} collective-permute-done((f32[16,8,128]{2,1,0:T(8,128)S(1)}, f32[16,8,128]{2,1,0:T(8,128)S(1)}, u32[]{:S(2)}, u32[]{:S(2)}) %collective-permute-start.4) | collective-permute-done | bytes 65568 | tf_op jit(solution)/shard_map/while/body/eval_jaxpr/ppermute | solution.py:23
  54.1 3.8 %collective-permute-done.2 = f32[16,8]{1,0:T(8,128)S(1)} collective-permute-done((f32[16,8]{1,0:T(8,128)S(1)}, f32[16,8]{1,0:T(8,128)S(1)}, u32[]{:S(2)}, u32[]{:S(2)}) %collective-permute-start.2) | collective-permute-done | bytes 544 | tf_op jit(solution)/shard_map/while/body/eval_jaxpr/ppermute | solution.py:23
  65.3 4.0 %collective-permute-done.4 = f32[16,8,128]{2,1,0:T(8,128)S(1)} collective-permute-done((f32[16,8,128]{2,1,0:T(8,128)S(1)}, f32[16,8,128]{2,1,0:T(8,128)S(1)}, u32[]{:S(2)}, u32[]{:S(2)}) %collective-permute-start.4) | collective-permute-done | bytes 65568 | tf_op jit(solution)/shard_map/while/body/eval_jaxpr/ppermute | solution.py:23
  71.4 3.7 %collective-permute-done.2 = f32[16,8]{1,0:T(8,128)S(1)} collective-permute-done((f32[16,8]{1,0:T(8,128)S(1)}, f32[16,8]{1,0:T(8,128)S(1)}, u32[]{:S(2)}, u32[]{:S(2)}) %collective-permute-start.2) | collective-permute-done | bytes 544 | tf_op jit(solution)/shard_map/while/body/eval_jaxpr/ppermute | solution.py:23
  83.1 4.0 %collective-permute-done.4 = f32[16,8,128]{2,1,0:T(8,128)S(1)} collective-permute-done((f32[16,8,128]{2,1,0:T(8,128)S(1)}, f32[16,8,128]{2,1,0:T(8,128)S(1)}, u32[]{:S(2)}, u32[]{:S(2)}) %collective-permute-start.4) | collective-permute-done | bytes 65568 | tf_op jit(solution)/shard_map/while/body/eval_jaxpr/ppermute | solution.py:23
  101.4 3.2 %collective-permute-done.4 = f32[16,8,128]{2,1,0:T(8,128)S(1)} collective-permute-done((f32[16,8,128]{2,1,0:T(8,128)S(1)}, f32[16,8,128]{2,1,0:T(8,128)S(1)}, u32[]{:S(2)}, u32[]{:S(2)}) %collective-permute-start.4) | collective-permute-done | bytes 65568 | tf_op jit(solution)/shard_map/while/body/eval_jaxpr/ppermute | solution.py:23
  119.0 3.2 %collective-permute-done.4 = f32[16,8,128]{2,1,0:T(8,128)S(1)} collective-permute-done((f32[16,8,128]{2,1,0:T(8,128)S(1)}, f32[16,8,128]{2,1,0:T(8,128)S(1)}, u32[]{:S(2)}, u32[]{:S(2)}) %collective-permute-start.4) | collective-permute-done | bytes 65568 | tf_op jit(solution)/shard_map/while/body/eval_jaxpr/ppermute | solution.py:23
  136.6 2.9 collective-permute-done.4
  153.8 3.4 %collective-permute-done.4 = f32[16,8,128]{2,1,0:T(8,128)S(1)} collective-permute-done((f32[16,8,128]{2,1,0:T(8,128)S(1)}, f32[16,8,128]{2,1,0:T(8,128)S(1)}, u32[]{:S(2)}, u32[]{:S(2)}) %collective-permute-start.4) | collective-permute-done | bytes 65568 | tf_op jit(solution)/shard_map/while/body/eval_jaxpr/ppermute | solution.py:23
  171.7 3.2 %collective-permute-done.4 = f32[16,8,128]{2,1,0:T(8,128)S(1)} collective-permute-done((f32[16,8,128]{2,1,0:T(8,128)S(1)}, f32[16,8,128]{2,1,0:T(8,128)S(1)}, u32[]{:S(2)}, u32[]{:S(2)}) %collective-permute-start.4) | collective-permute-done | bytes 65568 | tf_op jit(solution)/shard_map/while/body/eval_jaxpr/ppermute | solution.py:23
  189.3 3.2 %collective-permute-done.4 = f32[16,8,128]{2,1,0:T(8,128)S(1)} collective-permute-done((f32[16,8,128]{2,1,0:T(8,128)S(1)}, f32[16,8,128]{2,1,0:T(8,128)S(1)}, u32[]{:S(2)}, u32[]{:S(2)}) %collective-permute-start.4) | collective-permute-done | bytes 65568 | tf_op jit(solution)/shard_map/while/body/eval_jaxpr/ppermute | solution.py:23
  206.8 2.9 collective-permute-done.4
  224.1 3.4 %collective-permute-done.4 = f32[16,8,128]{2,1,0:T(8,128)S(1)} collective-permute-done((f32[16,8,128]{2,1,0:T(8,128)S(1)}, f32[16,8,128]{2,1,0:T(8,128)S(1)}, u32[]{:S(2)}, u32[]{:S(2)}) %collective-permute-start.4) | collective-permute-done | bytes 65568 | tf_op jit(solution)/shard_map/while/body/eval_jaxpr/ppermute | solution.py:23
  241.9 3.2 %collective-permute-done.4 = f32[16,8,128]{2,1,0:T(8,128)S(1)} collective-permute-done((f32[16,8,128]{2,1,0:T(8,128)S(1)}, f32[16,8,128]{2,1,0:T(8,128)S(1)}, u32[]{:S(2)}, u32[]{:S(2)}) %collective-permute-start.4) | collective-permute-done | bytes 65568 | tf_op jit(solution)/shard_map/while/body/eval_jaxpr/ppermute | solution.py:23
  259.5 3.2 %collective-permute-done.4 = f32[16,8,128]{2,1,0:T(8,128)S(1)} collective-permute-done((f32[16,8,128]{2,1,0:T(8,128)S(1)}, f32[16,8,128]{2,1,0:T(8,128)S(1)}, u32[]{:S(2)}, u32[]{:S(2)}) %collective-permute-start.4) | collective-permute-done | bytes 65568 | tf_op jit(solution)/shard_map/while/body/eval_jaxpr/ppermute | solution.py:23
  294.3 3.4 %collective-permute-done.4 = f32[16,8,128]{2,1,0:T(8,128)S(1)} collective-permute-done((f32[16,8,128]{2,1,0:T(8,128)S(1)}, f32[16,8,128]{2,1,0:T(8,128)S(1)}, u32[]{:S(2)}, u32[]{:S(2)}) %collective-permute-start.4) | collective-permute-done | bytes 65568 | tf_op jit(solution)/shard_map/while/body/eval_jaxpr/ppermute | solution.py:23
  299.6 4.6 %collective-permute-done.5 = bf16[16,8,128]{2,1,0:T(8,128)(2,1)} collective-permute-done((bf16[16,8,128]{2,1,0:T(8,128)(2,1)S(1)}, bf16[16,8,128]{2,1,0:T(8,128)(2,1)}, u32[]{:S(2)}, u32[]{:S(2)}) %collective-permute-start.5) | collective-permute-done | bytes 32800 | tf_op jit(solution)/shard_map/ppermute | solution.py:23
  304.1 3.3 %all-to-all-start.1 = ((bf16[16,8,128]{2,1,0:T(8,128)(2,1)}), bf16[16,8,128]{2,1,0:T(8,128)(2,1)S(1)}, u32[]{:S(2)}, u32[]{:S(2)}) async-start(bf16[16,8,128]{2,1,0:T(8,128)(2,1)} %collective-permute-done.5), calls=%async_computation.1 | async-start | bytes 65536 | tf_op jit(solution)/shard_map/all_to_all | solution.py:123
  308.5 7.0 %all-to-all-done.1 = bf16[16,8,128]{2,1,0:T(8,128)(2,1)S(1)} async-done(((bf16[16,8,128]{2,1,0:T(8,128)(2,1)}), bf16[16,8,128]{2,1,0:T(8,128)(2,1)S(1)}, u32[]{:S(2)}, u32[]{:S(2)}) %all-to-all-start.1) | async-done | bytes 32800 | tf_op jit(solution)/shard_map/all_to_all | solution.py:123
  (738 shorter events, 218.4 us)
Async XLA Ops:
  4.2 18.9 %all-to-all-start = ((f32[2,64,258]{2,0,1:T(2,128)}), f32[2,64,258]{2,0,1:T(2,128)S(1)}, u32[]{:S(2)}, u32[]{:S(2)}) async-start(f32[2,64,258]{2,0,1:T(2,128)} %copy.80), calls=%async_computation | async-start | bytes 393216 | tf_op jit(solution)/shard_map/all_to_all | solution.py:14
  24.2 7.0 %collective-permute-start = (bf16[16,8,128]{2,1,0:T(8,128)(2,1)S(1)}, bf16[16,8,128]{2,1,0:T(8,128)(2,1)S(1)}, u32[]{:S(2)}, u32[]{:S(2)}) collective-permute-start(bf16[16,8,128]{2,1,0:T(8,128)(2,1)S(1)} %copy.106), channel_id=1, source_target_pairs={{0,8},{8,16},{16,24},{24,32},{32,40},{40,48},{48,56},{56,64},{64,7... | collective-permute-start | bytes 98312 | tf_op jit(solution)/shard_map/while/body/eval_jaxpr/ppermute | solution.py:23
  24.2 7.0 %collective-permute-start.1 = (bf16[16,8,128]{2,1,0:T(8,128)(2,1)S(1)}, bf16[16,8,128]{2,1,0:T(8,128)(2,1)S(1)}, u32[]{:S(2)}, u32[]{:S(2)}) collective-permute-start(bf16[16,8,128]{2,1,0:T(8,128)(2,1)S(1)} %copy.107), channel_id=1, source_target_pairs={{0,8},{8,16},{16,24},{24,32},{32,40},{40,48},{48,56},{56,64},{64,7... | collective-permute-start | bytes 98312 | tf_op jit(solution)/shard_map/while/body/eval_jaxpr/ppermute | solution.py:23
  34.4 6.0 %collective-permute-start = (bf16[16,8,128]{2,1,0:T(8,128)(2,1)S(1)}, bf16[16,8,128]{2,1,0:T(8,128)(2,1)S(1)}, u32[]{:S(2)}, u32[]{:S(2)}) collective-permute-start(bf16[16,8,128]{2,1,0:T(8,128)(2,1)S(1)} %copy.106), channel_id=1, source_target_pairs={{0,8},{8,16},{16,24},{24,32},{32,40},{40,48},{48,56},{56,64},{64,7... | collective-permute-start | bytes 98312 | tf_op jit(solution)/shard_map/while/body/eval_jaxpr/ppermute | solution.py:23
  41.8 6.2 %collective-permute-start = (bf16[16,8,128]{2,1,0:T(8,128)(2,1)S(1)}, bf16[16,8,128]{2,1,0:T(8,128)(2,1)S(1)}, u32[]{:S(2)}, u32[]{:S(2)}) collective-permute-start(bf16[16,8,128]{2,1,0:T(8,128)(2,1)S(1)} %copy.106), channel_id=1, source_target_pairs={{0,8},{8,16},{16,24},{24,32},{32,40},{40,48},{48,56},{56,64},{64,7... | collective-permute-start | bytes 98312 | tf_op jit(solution)/shard_map/while/body/eval_jaxpr/ppermute | solution.py:23
  41.8 6.2 %collective-permute-start.1 = (bf16[16,8,128]{2,1,0:T(8,128)(2,1)S(1)}, bf16[16,8,128]{2,1,0:T(8,128)(2,1)S(1)}, u32[]{:S(2)}, u32[]{:S(2)}) collective-permute-start(bf16[16,8,128]{2,1,0:T(8,128)(2,1)S(1)} %copy.107), channel_id=1, source_target_pairs={{0,8},{8,16},{16,24},{24,32},{32,40},{40,48},{48,56},{56,64},{64,7... | collective-permute-start | bytes 98312 | tf_op jit(solution)/shard_map/while/body/eval_jaxpr/ppermute | solution.py:23
  52.0 6.0 %collective-permute-start = (bf16[16,8,128]{2,1,0:T(8,128)(2,1)S(1)}, bf16[16,8,128]{2,1,0:T(8,128)(2,1)S(1)}, u32[]{:S(2)}, u32[]{:S(2)}) collective-permute-start(bf16[16,8,128]{2,1,0:T(8,128)(2,1)S(1)} %copy.106), channel_id=1, source_target_pairs={{0,8},{8,16},{16,24},{24,32},{32,40},{40,48},{48,56},{56,64},{64,7... | collective-permute-start | bytes 98312 | tf_op jit(solution)/shard_map/while/body/eval_jaxpr/ppermute | solution.py:23
  59.2 6.1 %collective-permute-start = (bf16[16,8,128]{2,1,0:T(8,128)(2,1)S(1)}, bf16[16,8,128]{2,1,0:T(8,128)(2,1)S(1)}, u32[]{:S(2)}, u32[]{:S(2)}) collective-permute-start(bf16[16,8,128]{2,1,0:T(8,128)(2,1)S(1)} %copy.106), channel_id=1, source_target_pairs={{0,8},{8,16},{16,24},{24,32},{32,40},{40,48},{48,56},{56,64},{64,7... | collective-permute-start | bytes 98312 | tf_op jit(solution)/shard_map/while/body/eval_jaxpr/ppermute | solution.py:23
  59.2 6.1 %collective-permute-start.1 = (bf16[16,8,128]{2,1,0:T(8,128)(2,1)S(1)}, bf16[16,8,128]{2,1,0:T(8,128)(2,1)S(1)}, u32[]{:S(2)}, u32[]{:S(2)}) collective-permute-start(bf16[16,8,128]{2,1,0:T(8,128)(2,1)S(1)} %copy.107), channel_id=1, source_target_pairs={{0,8},{8,16},{16,24},{24,32},{32,40},{40,48},{48,56},{56,64},{64,7... | collective-permute-start | bytes 98312 | tf_op jit(solution)/shard_map/while/body/eval_jaxpr/ppermute | solution.py:23
  69.3 6.0 %collective-permute-start = (bf16[16,8,128]{2,1,0:T(8,128)(2,1)S(1)}, bf16[16,8,128]{2,1,0:T(8,128)(2,1)S(1)}, u32[]{:S(2)}, u32[]{:S(2)}) collective-permute-start(bf16[16,8,128]{2,1,0:T(8,128)(2,1)S(1)} %copy.106), channel_id=1, source_target_pairs={{0,8},{8,16},{16,24},{24,32},{32,40},{40,48},{48,56},{56,64},{64,7... | collective-permute-start | bytes 98312 | tf_op jit(solution)/shard_map/while/body/eval_jaxpr/ppermute | solution.py:23
  76.4 6.6 %collective-permute-start = (bf16[16,8,128]{2,1,0:T(8,128)(2,1)S(1)}, bf16[16,8,128]{2,1,0:T(8,128)(2,1)S(1)}, u32[]{:S(2)}, u32[]{:S(2)}) collective-permute-start(bf16[16,8,128]{2,1,0:T(8,128)(2,1)S(1)} %copy.106), channel_id=1, source_target_pairs={{0,8},{8,16},{16,24},{24,32},{32,40},{40,48},{48,56},{56,64},{64,7... | collective-permute-start | bytes 98312 | tf_op jit(solution)/shard_map/while/body/eval_jaxpr/ppermute | solution.py:23
  76.5 6.6 %collective-permute-start.1 = (bf16[16,8,128]{2,1,0:T(8,128)(2,1)S(1)}, bf16[16,8,128]{2,1,0:T(8,128)(2,1)S(1)}, u32[]{:S(2)}, u32[]{:S(2)}) collective-permute-start(bf16[16,8,128]{2,1,0:T(8,128)(2,1)S(1)} %copy.107), channel_id=1, source_target_pairs={{0,8},{8,16},{16,24},{24,32},{32,40},{40,48},{48,56},{56,64},{64,7... | collective-permute-start | bytes 98312 | tf_op jit(solution)/shard_map/while/body/eval_jaxpr/ppermute | solution.py:23
  87.0 6.0 %collective-permute-start = (bf16[16,8,128]{2,1,0:T(8,128)(2,1)S(1)}, bf16[16,8,128]{2,1,0:T(8,128)(2,1)S(1)}, u32[]{:S(2)}, u32[]{:S(2)}) collective-permute-start(bf16[16,8,128]{2,1,0:T(8,128)(2,1)S(1)} %copy.106), channel_id=1, source_target_pairs={{0,8},{8,16},{16,24},{24,32},{32,40},{40,48},{48,56},{56,64},{64,7... | collective-permute-start | bytes 98312 | tf_op jit(solution)/shard_map/while/body/eval_jaxpr/ppermute | solution.py:23
  104.7 6.0 %collective-permute-start = (bf16[16,8,128]{2,1,0:T(8,128)(2,1)S(1)}, bf16[16,8,128]{2,1,0:T(8,128)(2,1)S(1)}, u32[]{:S(2)}, u32[]{:S(2)}) collective-permute-start(bf16[16,8,128]{2,1,0:T(8,128)(2,1)S(1)} %copy.106), channel_id=1, source_target_pairs={{0,8},{8,16},{16,24},{24,32},{32,40},{40,48},{48,56},{56,64},{64,7... | collective-permute-start | bytes 98312 | tf_op jit(solution)/shard_map/while/body/eval_jaxpr/ppermute | solution.py:23
  122.2 6.0 %collective-permute-start = (bf16[16,8,128]{2,1,0:T(8,128)(2,1)S(1)}, bf16[16,8,128]{2,1,0:T(8,128)(2,1)S(1)}, u32[]{:S(2)}, u32[]{:S(2)}) collective-permute-start(bf16[16,8,128]{2,1,0:T(8,128)(2,1)S(1)} %copy.106), channel_id=1, source_target_pairs={{0,8},{8,16},{16,24},{24,32},{32,40},{40,48},{48,56},{56,64},{64,7... | collective-permute-start | bytes 98312 | tf_op jit(solution)/shard_map/while/body/eval_jaxpr/ppermute | solution.py:23
  130.6 6.0 %collective-permute-start = (bf16[16,8,128]{2,1,0:T(8,128)(2,1)S(1)}, bf16[16,8,128]{2,1,0:T(8,128)(2,1)S(1)}, u32[]{:S(2)}, u32[]{:S(2)}) collective-permute-start(bf16[16,8,128]{2,1,0:T(8,128)(2,1)S(1)} %copy.106), channel_id=1, source_target_pairs={{0,8},{8,16},{16,24},{24,32},{32,40},{40,48},{48,56},{56,64},{64,7... | collective-permute-start | bytes 98312 | tf_op jit(solution)/shard_map/while/body/eval_jaxpr/ppermute | solution.py:23
  139.5 6.0 %collective-permute-start = (bf16[16,8,128]{2,1,0:T(8,128)(2,1)S(1)}, bf16[16,8,128]{2,1,0:T(8,128)(2,1)S(1)}, u32[]{:S(2)}, u32[]{:S(2)}) collective-permute-start(bf16[16,8,128]{2,1,0:T(8,128)(2,1)S(1)} %copy.106), channel_id=1, source_target_pairs={{0,8},{8,16},{16,24},{24,32},{32,40},{40,48},{48,56},{56,64},{64,7... | collective-permute-start | bytes 98312 | tf_op jit(solution)/shard_map/while/body/eval_jaxpr/ppermute | solution.py:23
  147.9 6.0 %collective-permute-start = (bf16[16,8,128]{2,1,0:T(8,128)(2,1)S(1)}, bf16[16,8,128]{2,1,0:T(8,128)(2,1)S(1)}, u32[]{:S(2)}, u32[]{:S(2)}) collective-permute-start(bf16[16,8,128]{2,1,0:T(8,128)(2,1)S(1)} %copy.106), channel_id=1, source_target_pairs={{0,8},{8,16},{16,24},{24,32},{32,40},{40,48},{48,56},{56,64},{64,7... | collective-permute-start | bytes 98312 | tf_op jit(solution)/shard_map/while/body/eval_jaxpr/ppermute | solution.py:23
  192.5 6.0 %collective-permute-start = (bf16[16,8,128]{2,1,0:T(8,128)(2,1)S(1)}, bf16[16,8,128]{2,1,0:T(8,128)(2,1)S(1)}, u32[]{:S(2)}, u32[]{:S(2)}) collective-permute-start(bf16[16,8,128]{2,1,0:T(8,128)(2,1)S(1)} %copy.106), channel_id=1, source_target_pairs={{0,8},{8,16},{16,24},{24,32},{32,40},{40,48},{48,56},{56,64},{64,7... | collective-permute-start | bytes 98312 | tf_op jit(solution)/shard_map/while/body/eval_jaxpr/ppermute | solution.py:23
  209.7 6.0 %collective-permute-start = (bf16[16,8,128]{2,1,0:T(8,128)(2,1)S(1)}, bf16[16,8,128]{2,1,0:T(8,128)(2,1)S(1)}, u32[]{:S(2)}, u32[]{:S(2)}) collective-permute-start(bf16[16,8,128]{2,1,0:T(8,128)(2,1)S(1)} %copy.106), channel_id=1, source_target_pairs={{0,8},{8,16},{16,24},{24,32},{32,40},{40,48},{48,56},{56,64},{64,7... | collective-permute-start | bytes 98312 | tf_op jit(solution)/shard_map/while/body/eval_jaxpr/ppermute | solution.py:23
  227.5 6.0 %collective-permute-start = (bf16[16,8,128]{2,1,0:T(8,128)(2,1)S(1)}, bf16[16,8,128]{2,1,0:T(8,128)(2,1)S(1)}, u32[]{:S(2)}, u32[]{:S(2)}) collective-permute-start(bf16[16,8,128]{2,1,0:T(8,128)(2,1)S(1)} %copy.106), channel_id=1, source_target_pairs={{0,8},{8,16},{16,24},{24,32},{32,40},{40,48},{48,56},{56,64},{64,7... | collective-permute-start | bytes 98312 | tf_op jit(solution)/shard_map/while/body/eval_jaxpr/ppermute | solution.py:23
  245.1 6.0 %collective-permute-start = (bf16[16,8,128]{2,1,0:T(8,128)(2,1)S(1)}, bf16[16,8,128]{2,1,0:T(8,128)(2,1)S(1)}, u32[]{:S(2)}, u32[]{:S(2)}) collective-permute-start(bf16[16,8,128]{2,1,0:T(8,128)(2,1)S(1)} %copy.106), channel_id=1, source_target_pairs={{0,8},{8,16},{16,24},{24,32},{32,40},{40,48},{48,56},{56,64},{64,7... | collective-permute-start | bytes 98312 | tf_op jit(solution)/shard_map/while/body/eval_jaxpr/ppermute | solution.py:23
  253.5 6.0 %collective-permute-start = (bf16[16,8,128]{2,1,0:T(8,128)(2,1)S(1)}, bf16[16,8,128]{2,1,0:T(8,128)(2,1)S(1)}, u32[]{:S(2)}, u32[]{:S(2)}) collective-permute-start(bf16[16,8,128]{2,1,0:T(8,128)(2,1)S(1)} %copy.106), channel_id=1, source_target_pairs={{0,8},{8,16},{16,24},{24,32},{32,40},{40,48},{48,56},{56,64},{64,7... | collective-permute-start | bytes 98312 | tf_op jit(solution)/shard_map/while/body/eval_jaxpr/ppermute | solution.py:23
  304.1 11.3 %all-to-all-start.1 = ((bf16[16,8,128]{2,1,0:T(8,128)(2,1)}), bf16[16,8,128]{2,1,0:T(8,128)(2,1)S(1)}, u32[]{:S(2)}, u32[]{:S(2)}) async-start(bf16[16,8,128]{2,1,0:T(8,128)(2,1)} %collective-permute-done.5), calls=%async_computation.1 | async-start | bytes 65536 | tf_op jit(solution)/shard_map/all_to_all | solution.py:123
  (141 other events, 787.3 us)
where the time goes:
time: 317 us; the launch traced here: 316 us
  waiting for transfers between devices  177 us (56%)
  starting transfers between devices  78 us (25%)
  matrix products  46.4 us (15%)
  local copies, waits for them, and re-layouts  7.5 us (2%)
  other arithmetic  3.98 us (1%)
    ppermute x156, waiting for transfers between devices, shifted(): lax.ppermute(value, axis, [(i, (i + by) % peers) for i in range(peers)])  160 us
    ppermute x156, starting transfers between devices, shifted(): lax.ppermute(value, axis, [(i, (i + by) % peers) for i in range(peers)])  66.2 us
    dot_general x32, matrix products, block_terms(): jnp.einsum('rgk,rgd->kd', score_half, queries_in, preferred_element_type=...  11.4 us
    dot_general x32, matrix products, block_terms(): jnp.einsum('rgk,rgd->kd', weight_half, grads_in, preferred_element_type=j...  11.2 us
    all_to_all x1, waiting for transfers between devices, in_one_piece(): lax.all_to_all(both, axis, split_axis=split_dim, concat_axis=concat_dim,...  9.57 us
    dot_general x32, matrix products, block_terms(): jnp.einsum('rgd,kd->rgk', queries_in, key_rows, preferred_element_type=jn...  8.91 us
    all_to_all x1, starting transfers between devices, in_one_piece(): lax.all_to_all(both, axis, split_axis=split_dim, concat_axis=concat_dim,...  8.47 us
    dot_general x32, matrix products, block_terms(): jnp.einsum('rgd,kd->rgk', grads_in, value_rows, preferred_element_type=jn...  7.77 us
  transfers between devices with their start and end apart: 158, of which 96 were waited for; matrix products, arithmetic and copies ran while one was open for 16% of the time, Pallas kernels for 0%

commit v1 on v0

v1 whole, which is shorter than its diff:
```python
import functools
import math

import jax
import jax.numpy as jnp
from jax import lax
from jax.experimental import pallas as pl
from jax.experimental.pallas import tpu as pltpu
from jax.sharding import PartitionSpec as P

F32, BF16 = jnp.float32, jnp.bfloat16
MESH = pl.DeviceIdType.MESH

ROWS = 128
BLOCK = 2 * ROWS + 16
HALVES = {"all": (0, BLOCK), "a": (0, ROWS), "b": (ROWS, BLOCK - ROWS)}

CHUNKS = (
    (("o", (0, 0)), ("s", (0, 0))),
    (("o", (1, 0)), ("o", (3, 0))),
    (("s", (1, 0)), ("s", (3, 0))),
    (("o", (0, 1)), ("s", (0, 1))),
    (("o", (2, 0)), ("s", (2, 0))),
    (("o", (1, 1)), ("o", (1, 3))),
    (("o", (3, 1)), ("o", (3, 3))),
    (("s", (1, 1)), ("s", (1, 3))),
    (("s", (3, 1)), ("s", (3, 3))),
    (("o", (2, 1)), ("o", (2, 3))),
    (("s", (2, 1)), ("s", (2, 3))),
    (("o", (0, 2)), ("s", (0, 2))),
    (("o", (1, 2)), ("o", (3, 2))),
    (("s", (1, 2)), ("s", (3, 2))),
    (("o", (2, 2)), ("s", (2, 2))),
    (("o", (0, 3)), ("s", (0, 3))),
)
ARRIVE = {
    1: ((1, 0), (3, 0)),
    2: ((0, 1), (0, 3)),
    3: ((2, 0),),
    4: ((1, 1), (1, 3)),
    5: ((3, 1), (3, 3)),
    6: ((0, 2),),
    7: ((2, 1), (2, 3)),
    8: ((1, 2),),
    9: ((3, 2),),
    10: ((2, 2),),
}
SLOT = {name: 2 * c + i for c, pair in enumerate(CHUNKS) for i, name in enumerate(pair)}
CHUNK_OF = {name: c for c, pair in enumerate(CHUNKS) for name in pair}
PLACES = [(a, b) for a in range(4) for b in range(4)]
NUMBER = {place: i for i, place in enumerate(PLACES)}
MOVES = [((0, 0), (1, 0), "all", "p+"), ((0, 0), (3, 0), "all", "p-")]
MOVES += [((0, 0), (0, 1), "all", "q+"), ((0, 0), (0, 3), "all", "q-")]
MOVES += [((1, 0), (2, 0), "a", "p+"), ((3, 0), (2, 0), "b", "p-")]
for _a in (1, 3, 2):
    MOVES += [((_a, 0), (_a, 1), "all", "q+"), ((_a, 0), (_a, 3), "all", "q-")]
for _a in (0, 1, 3, 2):
    MOVES += [((_a, 1), (_a, 2), "a", "q+"), ((_a, 3), (_a, 2), "b", "q-")]
MOVES += [(place, place, "all", "sib") for place in PLACES]


def kernel(
    scaling,
    q_hbm, o_hbm, g_hbm, n_hbm, st_hbm, k_hbm, v_hbm,
    dq_ref, dk_hbm, dv_hbm,
    q_in, o_in, g_in, n_in, st_in, keys, vals, keys_t, jpos,
    stage, landed, blocks, part, part_half, part_in, total_half, total_in,
    dk_acc, dv_acc, dk_half, dv_half, fin, fin_in,
    in_sem, az_send, az_recv, mv_send, mv_recv, ps_send, ps_recv, tt_send, tt_recv,
    fz_send, fz_recv,
):
    s, k = lax.axis_index("seq"), lax.axis_index("kvh")
    x, y, core = s // 8, (s // 2) % 4, s % 2
    pa, pb = (1 - core) * x + core * y, (1 - core) * y + core * x

    def at(a, b):
        return (1 - core) * ((a * 4 + b) * 2) + core * ((b * 4 + a) * 2 + 1)

    sibling = s + 1 - 2 * core
    target = {
        "p+": at((pa + 1) % 4, pb),
        "p-": at((pa + 3) % 4, pb),
        "q+": at(pa, (pb + 1) % 4),
        "q-": at(pa, (pb + 3) % 4),
        "sib": sibling,
    }

    ins = [
        pltpu.make_async_copy(src, dst, in_sem.at[i])
        for i, (src, dst) in enumerate(
            (
                (g_hbm, g_in), (o_hbm, o_in), (n_hbm, n_in), (st_hbm, st_in), (q_hbm, q_in),
                (k_hbm, keys), (v_hbm, vals),
            )
        )
    ]
    for copy in ins:
        copy.start()

    barrier = pltpu.get_barrier_semaphore()
    for j in range(1, 8):
        pl.semaphore_signal(
            barrier, inc=1, device_id={"kvh": (k + j) % 8}, device_id_type=MESH
        )
    for a, b in PLACES[1:]:
        pl.semaphore_signal(
            barrier, inc=1, device_id={"seq": at((pa + a) % 4, (pb + b) % 4)}, device_id_type=MESH
        )
    pl.semaphore_signal(barrier, inc=1, device_id={"seq": sibling}, device_id_type=MESH)

    def move(n):
        source, dest, half, way = MOVES[n]
        first, count = HALVES[half]
        kind = "s" if way == "sib" else "o"
        return pltpu.make_async_remote_copy(
            src_ref=blocks.at[SLOT["o", source], pl.ds(first, count)],
            dst_ref=blocks.at[SLOT[kind, dest], pl.ds(first, count)],
            send_sem=mv_send.at[n],
            recv_sem=mv_recv.at[n],
            device_id={"seq": target[way]},
            device_id_type=MESH,
        )

    def pass_on(place):
        for n, m in enumerate(MOVES):
            if m[0] == place:
                move(n).start()

    def arrived(kind, place):
        for n, m in enumerate(MOVES):
            if m[1] == place and (m[3] == "sib") == (kind == "s"):
                move(n).wait_recv()

    def give_part(place):
        n = NUMBER[place]
        return pltpu.make_async_remote_copy(
            src_ref=part_half.at[SLOT["s", place]],
            dst_ref=part_in.at[n],
            send_sem=ps_send.at[n],
            recv_sem=ps_recv.at[n],
            device_id={"seq": sibling},
            device_id_type=MESH,
        )

    def give_total(place):
        n = NUMBER[place]
        a, b = place
        return pltpu.make_async_remote_copy(
            src_ref=total_half.at[n],
            dst_ref=total_in.at[n],
            send_sem=tt_send.at[n],
            recv_sem=tt_recv.at[n],
            device_id={"seq": at((pa - a + 4) % 4, (pb - b + 4) % 4)},
            device_id_type=MESH,
        )

    def combine(place):
        give_part(place).wait_recv()
        n = NUMBER[place]
        both = part[SLOT["o", place]] + part_in[n].astype(F32)
        if place == (0, 0):
            part[SLOT["o", place]] = both
        else:
            total_half[n] = both.astype(BF16)
            give_total(place).start()

    for copy in ins[:5]:
        copy.wait()
    heads = 8
    grads = g_in[...].astype(F32)
    queries = q_in[...].astype(F32)
    for j in range(8):
        rows = slice(heads * j, heads * (j + 1))
        stage[j, 0:16] = jnp.concatenate([queries[0, rows], queries[1, rows]], axis=0).astype(BF16)
        stage[j, 16:32] = jnp.concatenate([grads[0, rows], grads[1, rows]], axis=0).astype(BF16)
    product = (grads * o_in[...].astype(F32)).reshape(ROWS, 128)
    product_hi = product.astype(BF16)
    product_lo = (product - product_hi.astype(F32)).astype(BF16)
    ones = jnp.ones((16, 128), BF16)
    contract_last = (((1,), (1,)), ((), ()))
    delta = lax.dot_general(ones, product_hi, contract_last, preferred_element_type=F32)
    delta = delta + lax.dot_general(ones, product_lo, contract_last, preferred_element_type=F32)
    norm = n_in[...] * math.log2(math.e)
    norm = jnp.broadcast_to(
        jnp.concatenate([norm[0:1], norm[1:2]], axis=1), (16, 128)
    )

    row = lax.broadcasted_iota(jnp.int32, (16, 128), 0)
    lane = lax.broadcasted_iota(jnp.int32, (16, 128), 1)
    token = 16 * s + 2 * k
    start = jnp.where(lane < 64, st_in[token], st_in[token + 1])

    def parts_of(value):
        hi = value.astype(BF16).astype(F32)
        mid = (value - hi).astype(BF16).astype(F32)
        return hi, mid, value - hi - mid

    numbers = (
        *parts_of(norm),
        *parts_of(delta),
        (start // 128).astype(F32),
        (start % 128).astype(F32),
        jnp.full((16, 128), s, jnp.int32).astype(F32),
    )
    base = jnp.zeros((16, 128), F32)
    for i, value in enumerate(numbers):
        base = jnp.where(row == i, value, base)
    big_row = lax.broadcasted_iota(jnp.int32, (128, 128), 0)
    big_lane = lax.broadcasted_iota(jnp.int32, (128, 128), 1)
    spread = jnp.concatenate([base] * 8, axis=0)
    spread = jnp.where((big_lane % 64) // 8 == big_row // 16, spread, 0.0).astype(BF16)
    places = 16 * k + 8 * (big_row // 64) + big_row % 8
    pick = jnp.where(big_lane == places, 1.0, 0.0).astype(BF16)
    spread = jnp.dot(spread, pick, preferred_element_type=F32).astype(BF16)
    for j in range(8):
        stage[j, 32:48] = spread[16 * j : 16 * (j + 1)]

    pl.semaphore_wait(barrier, 7 + 15 + 1)

    def hand_out(j):
        peer = (k + j) % 8
        return pltpu.make_async_remote_copy(
            src_ref=stage.at[peer],
            dst_ref=landed.at[k],
            send_sem=az_send.at[j],
            recv_sem=az_recv.at[j],
            device_id={"kvh": peer},
            device_id_type=MESH,
        )

    def hand_in(j):
        return pltpu.make_async_remote_copy(
            src_ref=stage.at[(k + j) % 8],
            dst_ref=landed.at[(k + 8 - j) % 8],
            send_sem=az_send.at[j],
            recv_sem=az_recv.at[j],
            device_id={"kvh": (k + j) % 8},
            device_id_type=MESH,
        )

    for j in (4, 3, 5, 2, 6, 1, 7):
        hand_out(j).start()
    landed[k] = stage[k]
    key_count = keys.shape[0]
    for copy in ins[5:]:
        copy.wait()
    keys_t[...] = keys[...].astype(F32).T.astype(BF16)
    is_last = jnp.where(s == 31, 1.0, 0.0).astype(F32)
    sign = 1.0 - 2.0 * is_last
    jpos[...] = sign * lax.broadcasted_iota(jnp.int32, (key_count, 128), 0).astype(F32)
    dk_acc[...] = jnp.zeros_like(dk_acc)
    dv_acc[...] = jnp.zeros_like(dv_acc)
    for j in range(1, 8):
        hand_in(j).wait_recv()
    mine = SLOT["o", (0, 0)]
    aux = jnp.zeros((16, 128), F32)
    for j in range(8):
        blocks[mine, 16 * j : 16 * (j + 1)] = landed[j, 0:16]
        blocks[mine, ROWS + 16 * j : ROWS + 16 * (j + 1)] = landed[j, 16:32]
        aux = aux + landed[j, 32:48].astype(F32)
    blocks[mine, 2 * ROWS : BLOCK] = aux.astype(BF16)
    pass_on((0, 0))

    shift = (s * key_count).astype(F32)
    in_block = (lax.broadcasted_iota(jnp.int32, (1, 256), 1) % 128) // 8
    last_bound = -(512.0 + in_block.astype(F32))
    factor = scaling * math.log2(math.e)
    tile = 256

    def chunk_step(c, carry):
        for at_chunk in range(16):
            def events(at_chunk=at_chunk):
                for place in ARRIVE.get(at_chunk, ()):
                    arrived("o", place)
                    pass_on(place)
                for kind, place in CHUNKS[at_chunk]:
                    if kind == "s":
                        arrived("s", place)
                for place in PLACES:
                    if CHUNK_OF["s", place] + 2 == at_chunk:
                        combine(place)

            pl.when(c == at_chunk)(events)

        aux = jnp.concatenate(
            [blocks[2 * c + i, 2 * ROWS : BLOCK].astype(F32) for i in range(2)], axis=1
        )
        norm = aux[0:1] + aux[1:2] + aux[2:3]
        delta = aux[3:4] + aux[4:5] + aux[5:6]
        first = aux[6:7] * 128.0 + aux[7:8] - shift
        bound = jnp.where(is_last > 0.5, last_bound - 16.0 * aux[8:9], first)
        q = blocks[pl.ds(2 * c, 2), 0:ROWS].reshape(2 * ROWS, 128)
        g = blocks[pl.ds(2 * c, 2), ROWS : 2 * ROWS].reshape(2 * ROWS, 128)
        dq = jnp.zeros((128, 2 * ROWS), F32)
        for t in range(key_count // tile):
            here = slice(t * tile, (t + 1) * tile)
            scores = lax.dot_general(keys[here], q, contract_last, preferred_element_type=F32)
            pos = jpos[here]
            pos = jnp.concatenate([pos, pos], axis=1)
            weights = jnp.where(pos >= bound, jnp.exp2(scores * factor - norm), 0.0)
            grads = lax.dot_general(vals[here], g, contract_last, preferred_element_type=F32)
            score_half = (weights * (grads - delta)).astype(BF16)
            dv_acc[here] += jnp.dot(weights.astype(BF16), g, preferred_element_type=F32)
            dk_acc[here] += jnp.dot(score_half, q, preferred_element_type=F32)
            dq = dq + jnp.dot(keys_t[:, here], score_half, preferred_element_type=F32)
        for i in range(2):
            mine = dq[:, i * ROWS : (i + 1) * ROWS]
            part[2 * c + i] = mine
            part_half[2 * c + i] = mine.astype(BF16)

        for at_chunk in range(16):
            def give(at_chunk=at_chunk):
                for kind, place in CHUNKS[at_chunk]:
                    if kind == "s":
                        give_part(place).start()

            if any(kind == "s" for kind, _ in CHUNKS[at_chunk]):
                pl.when(c == at_chunk)(give)
        return carry

    lax.fori_loop(0, 16, chunk_step, 0)

    late = [place for place in PLACES if CHUNK_OF["s", place] + 2 > 15]
    late = sorted(late, key=lambda place: CHUNK_OF["s", place])
    for place in late[:-1]:
        combine(place)
    dk_half[...] = (dk_acc[...] * scaling).astype(BF16)
    out_k = pltpu.make_async_copy(dk_half, dk_hbm, in_sem.at[0])
    out_k.start()
    combine(late[-1])
    dv_half[...] = dv_acc[...].astype(BF16)
    out_v = pltpu.make_async_copy(dv_half, dv_hbm, in_sem.at[1])
    out_v.start()

    total = part[SLOT["o", (0, 0)]]
    for place in PLACES[1:]:
        give_total(place).wait_recv()
        total = total + total_in[NUMBER[place]].astype(F32)
    fin[...] = (total.T * scaling).astype(BF16)

    def send_back(j):
        peer = (k + j) % 8
        return pltpu.make_async_remote_copy(
            src_ref=fin.at[pl.ds(pl.multiple_of(16 * peer, 16), 16)],
            dst_ref=fin_in.at[k],
            send_sem=fz_send.at[j],
            recv_sem=fz_recv.at[j],
            device_id={"kvh": peer},
            device_id_type=MESH,
        )

    def come_back(j):
        peer = (k + j) % 8
        return pltpu.make_async_remote_copy(
            src_ref=fin.at[pl.ds(pl.multiple_of(16 * peer, 16), 16)],
            dst_ref=fin_in.at[(k + 8 - j) % 8],
            send_sem=fz_send.at[j],
            recv_sem=fz_recv.at[j],
            device_id={"kvh": peer},
            device_id_type=MESH,
        )

    for j in (4, 3, 5, 2, 6, 1, 7):
        send_back(j).start()
    fin_in[k] = fin[pl.ds(pl.multiple_of(16 * k, 16), 16)]

    for n in range(len(MOVES)):
        move(n).wait_send()
    for place in PLACES:
        give_part(place).wait_send()
        if place != (0, 0):
            give_total(place).wait_send()
    for j in range(1, 8):
        hand_out(j).wait_send()
    for j in range(1, 8):
        come_back(j).wait_recv()
    both = [fin_in[j].astype(F32) for j in range(8)]
    for t in range(2):
        rows = [b[8 * t : 8 * (t + 1)] for b in both]
        dq_ref[t] = jnp.concatenate(rows, axis=0).astype(BF16)
    for j in range(1, 8):
        send_back(j).wait_send()
    out_k.wait()
    out_v.wait()


def local(queries, attn_out, grad_out, log_norms, query_starts, keys, values):
    scaling = queries.shape[-1] ** (-0.5)
    key_count = keys.shape[0]
    anywhere = pl.BlockSpec(memory_space=pl.ANY)
    sems = [7, 8, 8, len(MOVES), len(MOVES), 16, 16, 16, 16, 8, 8]
    dq, dk, dv = pl.pallas_call(
        functools.partial(kernel, scaling),
        out_shape=(
            jax.ShapeDtypeStruct((2, 64, 128), BF16),
            jax.ShapeDtypeStruct((key_count, 128), BF16),
            jax.ShapeDtypeStruct((key_count, 128), BF16),
        ),
        in_specs=[anywhere] * 7,
        out_specs=(pl.BlockSpec(memory_space=pltpu.VMEM), anywhere, anywhere),
        scratch_shapes=[
            pltpu.VMEM((2, 64, 128), BF16),
            pltpu.VMEM((2, 64, 128), BF16),
            pltpu.VMEM((2, 64, 128), BF16),
            pltpu.VMEM((2, 64), F32),
            pltpu.SMEM((512,), jnp.int32),
            pltpu.VMEM((key_count, 128), BF16),
            pltpu.VMEM((key_count, 128), BF16),
            pltpu.VMEM((128, key_count), BF16),
            pltpu.VMEM((key_count, 128), F32),
            pltpu.VMEM((8, 48, 128), BF16),
            pltpu.VMEM((8, 48, 128), BF16),
            pltpu.VMEM((32, BLOCK, 128), BF16),
            pltpu.VMEM((32, 128, ROWS), F32),
            pltpu.VMEM((32, 128, ROWS), BF16),
            pltpu.VMEM((16, 128, ROWS), BF16),
            pltpu.VMEM((16, 128, ROWS), BF16),
            pltpu.VMEM((16, 128, ROWS), BF16),
            pltpu.VMEM((key_count, 128), F32),
            pltpu.VMEM((key_count, 128), F32),
            pltpu.VMEM((key_count, 128), BF16),
            pltpu.VMEM((key_count, 128), BF16),
            pltpu.VMEM((ROWS, 128), BF16),
            pltpu.VMEM((8, 16, 128), BF16),
            *[pltpu.SemaphoreType.DMA((n,)) for n in sems],
        ],
        cost_estimate=pl.CostEstimate(
            flops=10 * 4096 * key_count * 128,
            bytes_accessed=4 * key_count * 256,
            transcendentals=4096 * key_count,
        ),
        compiler_params=pltpu.CompilerParams(
            collective_id=0, has_side_effects=True, vmem_limit_bytes=40 * 1024 * 1024
        ),
    )(
        queries, attn_out, grad_out, log_norms, query_starts,
        keys.reshape(key_count, 128), values.reshape(key_count, 128),
    )
    return dq, dk[:, None, :], dv[:, None, :]


def solution(mesh):
    return jax.shard_map(
        local,
        mesh=mesh,
        in_specs=(
            P(("seq", "kvh"), None, None),
            P(("seq", "kvh"), None, None),
            P(("seq", "kvh"), None, None),
            P(("seq", "kvh"), None),
            P(),
            P("seq", "kvh", None),
            P("seq", "kvh", None),
        ),
        out_specs=(P(("seq", "kvh"), None, None), P("seq", "kvh", None), P("seq", "kvh", None)),
        check_vma=False,
    )
```

time: 317 us -> 58.1 us (0.18)
  waiting for transfers between devices: 177 us -> 0 us
  starting transfers between devices: 78 us -> 0 us
  Pallas kernels: 0 us -> 50.2 us
  matrix products: 46.4 us -> 0 us
  other arithmetic: 3.98 us -> 0 us
    ppermute x156 -> x0, waiting for transfers between devices: 160 us -> none  [shifted(): lax.ppermute(value, axis, [(i, (i + by) % peers) for i in range(peers)])]
    ppermute x156 -> x0, starting transfers between devices: 66.2 us -> none  [shifted(): lax.ppermute(value, axis, [(i, (i + by) % peers) for i in range(peers)])]
    pallas_call x0 -> x1, Pallas kernels: none -> 50.2 us  [local(): pl.pallas_call(functools.partial(kernel, scaling), out_shape=(jax.ShapeDt...]
    dot_general x160 -> x0, matrix products: 46.4 us -> none  [the longest x32 11.4 us: block_terms(): jnp.einsum('rgk,rgd->kd', score_half, queries_in, preferred_element_type=...]
    all_to_all x2 -> x0, waiting for transfers between devices: 16.5 us -> none  [the longest x1 9.57 us: in_one_piece(): lax.all_to_all(both, axis, split_axis=split_dim, concat_axis=concat_dim,...]
    all_to_all x2 -> x0, starting transfers between devices: 11.8 us -> none  [the longest x1 8.47 us: in_one_piece(): lax.all_to_all(both, axis, split_axis=split_dim, concat_axis=concat_dim,...]
    unnamed x15 -> x17, local copies, waits for them, and re-layouts: 2.28 us -> 6.87 us
  transfers between devices with their start and end apart: 158 -> 0, of which waited for: 96 -> 0; matrix products, arithmetic and copies ran while one was open for 16% -> 0% of each run, Pallas kernels for 0% -> 0%
where the time goes in v1:
time: 58.1 us; the launch traced here: 57.8 us
  Pallas kernels  50.2 us (86%)
  local copies, waits for them, and re-layouts  6.87 us (12%)
  between operations  0.66 us (1%)
    pallas_call x1, Pallas kernels, local(): pl.pallas_call(functools.partial(kernel, scaling), out_shape=(jax.ShapeDt...  50.2 us
    unnamed x17, local copies, waits for them, and re-layouts  6.87 us

profile of v1, /device:TPU:2, one launch (start us, length us, event | category | flops | bytes accessed | tf_op | source)
XLA Modules:
  0.0 57.8 jit_solution(9612016941073140153)
XLA Ops:
  0.6 0.0 copy-start.5
  0.6 0.0 copy-start.6
  0.7 0.7 %copy-done.5 = s32[512]{0:T(512)S(1)} copy-done((s32[512]{0:T(512)S(1)}, s32[512]{0:T(512)}, u32[]{:S(2)}) %copy-start.5) | copy-done | bytes 2072
  1.3 0.0 copy-done.6
  1.3 0.0 copy-start
  1.3 0.9 %copy-done = bf16[1024,1,128]{2,0,1:T(8,128)(2,1)S(1)} copy-done((bf16[1024,1,128]{2,0,1:T(8,128)(2,1)S(1)}, bf16[1024,1,128]{2,0,1:T(8,128)(2,1)}, u32[]{:S(2)}) %copy-start) | copy-done | bytes 262168
  2.3 0.0 copy-start.1
  2.3 0.9 %copy-done.1 = bf16[1024,1,128]{2,0,1:T(8,128)(2,1)S(1)} copy-done((bf16[1024,1,128]{2,0,1:T(8,128)(2,1)S(1)}, bf16[1024,1,128]{2,0,1:T(8,128)(2,1)}, u32[]{:S(2)}) %copy-start.1) | copy-done | bytes 262168
  3.2 0.0 copy-start.2
  3.2 0.8 %copy-done.2 = bf16[2,64,128]{2,1,0:T(8,128)(2,1)S(1)} copy-done((bf16[2,64,128]{2,1,0:T(8,128)(2,1)S(1)}, bf16[2,64,128]{2,1,0:T(8,128)(2,1)}, u32[]{:S(2)}) %copy-start.2) | copy-done | bytes 32792
  4.0 0.0 copy-start.3
  4.0 0.8 %copy-done.3 = bf16[2,64,128]{2,1,0:T(8,128)(2,1)S(1)} copy-done((bf16[2,64,128]{2,1,0:T(8,128)(2,1)S(1)}, bf16[2,64,128]{2,1,0:T(8,128)(2,1)}, u32[]{:S(2)}) %copy-start.3) | copy-done | bytes 32792
  4.7 0.0 copy-start.4
  4.7 0.8 %copy-done.4 = bf16[2,64,128]{2,1,0:T(8,128)(2,1)S(1)} copy-done((bf16[2,64,128]{2,1,0:T(8,128)(2,1)S(1)}, bf16[2,64,128]{2,1,0:T(8,128)(2,1)}, u32[]{:S(2)}) %copy-start.4) | copy-done | bytes 32792
  5.5 50.2 %shard_map.94 = (bf16[2,64,128]{2,1,0:T(8,128)(2,1)S(1)}, bf16[1024,128]{1,0:T(8,128)(2,1)S(1)}, bf16[1024,128]{1,0:T(8,128)(2,1)S(1)}) custom-call(bf16[2,64,128]{2,1,0:T(8,128)(2,1)S(1)} %copy-done.2, bf16[2,64,128]{2,1,0:T(8,128)(2,1)S(1)} %copy-done.3, bf16[2,64,128]{2,1,0:T(8,128)(2,1)S(1)} %copy-done.4, f32[2,64]{1,0:T(2,128)S(1)} %copy-done.6, ...), custom_call_target="tpu_custom_call" | custom-call | flops 5368709120 | bytes 1048576 | tf_op jit(solution)/shard_map/pallas_call | solution.py:392
  55.7 0.6 %copy.13 = bf16[2,64,128]{2,1,0:T(8,128)(2,1)} copy(bf16[2,64,128]{2,1,0:T(8,128)(2,1)S(1)} %get-tuple-element.12) | data formatting | bytes 65536
  56.4 0.7 %copy.14 = bf16[1024,1,128]{2,0,1:T(8,128)(2,1)} copy(bf16[1024,1,128]{2,0,1:T(8,128)(2,1)S(1)} %bitcast.5) | data formatting | bytes 524288
  57.1 0.7 %copy.15 = bf16[1024,1,128]{2,0,1:T(8,128)(2,1)} copy(bf16[1024,1,128]{2,0,1:T(8,128)(2,1)S(1)} %bitcast.4) | data formatting | bytes 524288
Async XLA Ops:
  0.6 0.7 %copy-start.5 = (s32[512]{0:T(512)S(1)}, s32[512]{0:T(512)}, u32[]{:S(2)}) copy-start(s32[512]{0:T(512)} %st_hbm.1) | copy-start | bytes 6148
  0.6 0.7 %copy-start.6 = (f32[2,64]{1,0:T(2,128)S(1)}, f32[2,64]{1,0:T(2,128)}, u32[]{:S(2)}) copy-start(f32[2,64]{1,0:T(2,128)} %n_hbm.1) | copy-start | bytes 1540
  1.3 0.9 %copy-start = (bf16[1024,1,128]{2,0,1:T(8,128)(2,1)S(1)}, bf16[1024,1,128]{2,0,1:T(8,128)(2,1)}, u32[]{:S(2)}) copy-start(bf16[1024,1,128]{2,0,1:T(8,128)(2,1)} %param.12) | copy-start | bytes 786436
  2.3 0.9 %copy-start.1 = (bf16[1024,1,128]{2,0,1:T(8,128)(2,1)S(1)}, bf16[1024,1,128]{2,0,1:T(8,128)(2,1)}, u32[]{:S(2)}) copy-start(bf16[1024,1,128]{2,0,1:T(8,128)(2,1)} %param.13) | copy-start | bytes 786436
  3.2 0.8 %copy-start.2 = (bf16[2,64,128]{2,1,0:T(8,128)(2,1)S(1)}, bf16[2,64,128]{2,1,0:T(8,128)(2,1)}, u32[]{:S(2)}) copy-start(bf16[2,64,128]{2,1,0:T(8,128)(2,1)} %q_hbm.1) | copy-start | bytes 98308
  4.0 0.8 %copy-start.3 = (bf16[2,64,128]{2,1,0:T(8,128)(2,1)S(1)}, bf16[2,64,128]{2,1,0:T(8,128)(2,1)}, u32[]{:S(2)}) copy-start(bf16[2,64,128]{2,1,0:T(8,128)(2,1)} %o_hbm.1) | copy-start | bytes 98308
  4.7 0.8 %copy-start.4 = (bf16[2,64,128]{2,1,0:T(8,128)(2,1)S(1)}, bf16[2,64,128]{2,1,0:T(8,128)(2,1)}, u32[]{:S(2)}) copy-start(bf16[2,64,128]{2,1,0:T(8,128)(2,1)} %g_hbm.1) | copy-start | bytes 98308

commit v2 on v1

--- a/solution.py
+++ b/solution.py
@@ -13,50 +13,44 @@
 
 ROWS = 128
 BLOCK = 2 * ROWS + 16
-HALVES = {"all": (0, BLOCK), "a": (0, ROWS), "b": (ROWS, BLOCK - ROWS)}
-
 CHUNKS = (
     (("o", (0, 0)), ("s", (0, 0))),
     (("o", (1, 0)), ("o", (3, 0))),
+    (("o", (0, 1)), ("o", (0, 3))),
     (("s", (1, 0)), ("s", (3, 0))),
-    (("o", (0, 1)), ("s", (0, 1))),
-    (("o", (2, 0)), ("s", (2, 0))),
+    (("o", (2, 0)), ("o", (0, 2))),
+    (("s", (2, 0)), ("s", (0, 2))),
     (("o", (1, 1)), ("o", (1, 3))),
     (("o", (3, 1)), ("o", (3, 3))),
     (("s", (1, 1)), ("s", (1, 3))),
+    (("o", (1, 2)), ("o", (3, 2))),
+    (("o", (2, 1)), ("o", (2, 3))),
+    (("o", (2, 2)), ("s", (2, 2))),
+    (("s", (1, 2)), ("s", (3, 2))),
+    (("s", (2, 1)), ("s", (2, 3))),
     (("s", (3, 1)), ("s", (3, 3))),
-    (("o", (2, 1)), ("o", (2, 3))),
-    (("s", (2, 1)), ("s", (2, 3))),
-    (("o", (0, 2)), ("s", (0, 2))),
-    (("o", (1, 2)), ("o", (3, 2))),
-    (("s", (1, 2)), ("s", (3, 2))),
-    (("o", (2, 2)), ("s", (2, 2))),
-    (("o", (0, 3)), ("s", (0, 3))),
+    (("s", (0, 1)), ("s", (0, 3))),
 )
 ARRIVE = {
     1: ((1, 0), (3, 0)),
-    2: ((0, 1), (0, 3)),
-    3: ((2, 0),),
-    4: ((1, 1), (1, 3)),
-    5: ((3, 1), (3, 3)),
-    6: ((0, 2),),
-    7: ((2, 1), (2, 3)),
-    8: ((1, 2),),
-    9: ((3, 2),),
-    10: ((2, 2),),
+    2: ((2, 0), (0, 1), (0, 3)),
+    4: ((0, 2),),
+    6: ((1, 1), (1, 3)),
+    7: ((3, 1), (3, 3)),
+    9: ((1, 2), (3, 2)),
+    10: ((2, 1), (2, 3), (2, 2)),
 }
+LAG = 4
 SLOT = {name: 2 * c + i for c, pair in enumerate(CHUNKS) for i, name in enumerate(pair)}
 CHUNK_OF = {name: c for c, pair in enumerate(CHUNKS) for name in pair}
 PLACES = [(a, b) for a in range(4) for b in range(4)]
 NUMBER = {place: i for i, place in enumerate(PLACES)}
-MOVES = [((0, 0), (1, 0), "all", "p+"), ((0, 0), (3, 0), "all", "p-")]
-MOVES += [((0, 0), (0, 1), "all", "q+"), ((0, 0), (0, 3), "all", "q-")]
-MOVES += [((1, 0), (2, 0), "a", "p+"), ((3, 0), (2, 0), "b", "p-")]
-for _a in (1, 3, 2):
-    MOVES += [((_a, 0), (_a, 1), "all", "q+"), ((_a, 0), (_a, 3), "all", "q-")]
-for _a in (0, 1, 3, 2):
-    MOVES += [((_a, 1), (_a, 2), "a", "q+"), ((_a, 3), (_a, 2), "b", "q-")]
-MOVES += [(place, place, "all", "sib") for place in PLACES]
+MOVES = []
+for _d in [(1, 0), (3, 0), (2, 0), (1, 1), (1, 3), (3, 1), (3, 3), (0, 2), (0, 1), (0, 3)]:
+    MOVES += [((0, 0), _d, _d)]
+for _s, _d in [((1, 0), (1, 2)), ((3, 0), (3, 2)), ((2, 0), (2, 2)), ((2, 0), (2, 1)), ((2, 0), (2, 3))]:
+    MOVES += [(_s, _d, (0, _d[1]))]
+MOVES = [(place, place, "sib") for place in PLACES] + MOVES
 
 
 def kernel(
@@ -65,7 +59,7 @@
     dq_ref, dk_hbm, dv_hbm,
     q_in, o_in, g_in, n_in, st_in, keys, vals, keys_t, jpos,
     stage, landed, blocks, part, part_half, part_in, total_half, total_in,
-    dk_acc, dv_acc, dk_half, dv_half, fin, fin_in,
+    score_buf, weight_buf, dk_half, dv_half, fin, fin_in,
     in_sem, az_send, az_recv, mv_send, mv_recv, ps_send, ps_recv, tt_send, tt_recv,
     fz_send, fz_recv,
 ):
@@ -78,12 +72,10 @@
 
     sibling = s + 1 - 2 * core
     target = {
-        "p+": at((pa + 1) % 4, pb),
-        "p-": at((pa + 3) % 4, pb),
-        "q+": at(pa, (pb + 1) % 4),
-        "q-": at(pa, (pb + 3) % 4),
         "sib": sibling,
     }
+    for a, b in PLACES[1:]:
+        target[a, b] = at((pa + a) % 4, (pb + b) % 4)
 
     ins = [
         pltpu.make_async_copy(src, dst, in_sem.at[i])
@@ -109,12 +101,11 @@
     pl.semaphore_signal(barrier, inc=1, device_id={"seq": sibling}, device_id_type=MESH)
 
     def move(n):
-        source, dest, half, way = MOVES[n]
-        first, count = HALVES[half]
+        source, dest, way = MOVES[n]
         kind = "s" if way == "sib" else "o"
         return pltpu.make_async_remote_copy(
-            src_ref=blocks.at[SLOT["o", source], pl.ds(first, count)],
-            dst_ref=blocks.at[SLOT[kind, dest], pl.ds(first, count)],
+            src_ref=blocks.at[SLOT["o", source]],
+            dst_ref=blocks.at[SLOT[kind, dest]],
             send_sem=mv_send.at[n],
             recv_sem=mv_recv.at[n],
             device_id={"seq": target[way]},
@@ -128,7 +119,7 @@
 
     def arrived(kind, place):
         for n, m in enumerate(MOVES):
-            if m[1] == place and (m[3] == "sib") == (kind == "s"):
+            if m[1] == place and (m[2] == "sib") == (kind == "s"):
                 move(n).wait_recv()
 
     def give_part(place):
@@ -248,8 +239,6 @@
     is_last = jnp.where(s == 31, 1.0, 0.0).astype(F32)
     sign = 1.0 - 2.0 * is_last
     jpos[...] = sign * lax.broadcasted_iota(jnp.int32, (key_count, 128), 0).astype(F32)
-    dk_acc[...] = jnp.zeros_like(dk_acc)
-    dv_acc[...] = jnp.zeros_like(dv_acc)
     for j in range(1, 8):
         hand_in(j).wait_recv()
     mine = SLOT["o", (0, 0)]
@@ -267,21 +256,52 @@
     factor = scaling * math.log2(math.e)
     tile = 256
 
+    def rows_of(c, first):
+        return blocks[pl.ds(2 * c, 2), first : first + ROWS].reshape(2 * ROWS, 128)
+
+    def query_part(c):
+        dq = jnp.dot(keys_t[...], score_buf[c], preferred_element_type=F32)
+        for i in range(2):
+            mine = dq[:, i * ROWS : (i + 1) * ROWS]
+            part[2 * c + i] = mine
+            part_half[2 * c + i] = mine.astype(BF16)
+
+    def events(at_chunk):
+        for place in ARRIVE.get(at_chunk, ()):
+            arrived("o", place)
+            pass_on(place)
+        for kind, place in CHUNKS[at_chunk]:
+            if kind == "s":
+                arrived("s", place)
+        for place in PLACES:
+            if CHUNK_OF["s", place] + LAG == at_chunk:
+                combine(place)
+
+    def give(at_chunk):
+        if at_chunk:
+            for kind, place in CHUNKS[at_chunk - 1]:
+                if kind == "s":
+                    give_part(place).start()
+
+    def by_chunk(c, low, high, do):
+        if high - low == 1:
+            do(low)
+            return
+        middle = (low + high) // 2
+
+        def lower():
+            by_chunk(c, low, middle, do)
+
+        def upper():
+            by_chunk(c, middle, high, do)
+
+        lax.cond(c < middle, lower, upper)
+
     def chunk_step(c, carry):
-        for at_chunk in range(16):
-            def events(at_chunk=at_chunk):
-                for place in ARRIVE.get(at_chunk, ()):
-                    arrived("o", place)
-                    pass_on(place)
-                for kind, place in CHUNKS[at_chunk]:
-                    if kind == "s":
-                        arrived("s", place)
-                for place in PLACES:
-                    if CHUNK_OF["s", place] + 2 == at_chunk:
-                        combine(place)
-
-            pl.when(c == at_chunk)(events)
-
+        by_chunk(c, 0, 16, events)
+
+        before = jnp.maximum(c - 1, 0)
+        query_part(before)
         aux = jnp.concatenate(
             [blocks[2 * c + i, 2 * ROWS : BLOCK].astype(F32) for i in range(2)], axis=1
         )
@@ -289,9 +309,7 @@
         delta = aux[3:4] + aux[4:5] + aux[5:6]
         first = aux[6:7] * 128.0 + aux[7:8] - shift
         bound = jnp.where(is_last > 0.5, last_bound - 16.0 * aux[8:9], first)
-        q = blocks[pl.ds(2 * c, 2), 0:ROWS].reshape(2 * ROWS, 128)
-        g = blocks[pl.ds(2 * c, 2), ROWS : 2 * ROWS].reshape(2 * ROWS, 128)
-        dq = jnp.zeros((128, 2 * ROWS), F32)
+        q, g = rows_of(c, 0), rows_of(c, ROWS)
         for t in range(key_count // tile):
             here = slice(t * tile, (t + 1) * tile)
             scores = lax.dot_general(keys[here], q, contract_last, preferred_element_type=F32)
@@ -299,36 +317,45 @@
             pos = jnp.concatenate([pos, pos], axis=1)
             weights = jnp.where(pos >= bound, jnp.exp2(scores * factor - norm), 0.0)
             grads = lax.dot_general(vals[here], g, contract_last, preferred_element_type=F32)
-            score_half = (weights * (grads - delta)).astype(BF16)
-            dv_acc[here] += jnp.dot(weights.astype(BF16), g, preferred_element_type=F32)
-            dk_acc[here] += jnp.dot(score_half, q, preferred_element_type=F32)
-            dq = dq + jnp.dot(keys_t[:, here], score_half, preferred_element_type=F32)
-        for i in range(2):
-            mine = dq[:, i * ROWS : (i + 1) * ROWS]
-            part[2 * c + i] = mine
-            part_half[2 * c + i] = mine.astype(BF16)
-
-        for at_chunk in range(16):
-            def give(at_chunk=at_chunk):
-                for kind, place in CHUNKS[at_chunk]:
-                    if kind == "s":
-                        give_part(place).start()
-
-            if any(kind == "s" for kind, _ in CHUNKS[at_chunk]):
-                pl.when(c == at_chunk)(give)
+            weight_buf[c, here] = weights.astype(BF16)
+            score_buf[c, here] = (weights * (grads - delta)).astype(BF16)
+
+        by_chunk(c, 0, 16, give)
         return carry
 
+    score_buf[0] = jnp.zeros(score_buf.shape[1:], BF16)
     lax.fori_loop(0, 16, chunk_step, 0)
-
-    late = [place for place in PLACES if CHUNK_OF["s", place] + 2 > 15]
+    query_part(15)
+    for kind, place in CHUNKS[15]:
+        if kind == "s":
+            give_part(place).start()
+
+    late = [place for place in PLACES if CHUNK_OF["s", place] + LAG > 15]
     late = sorted(late, key=lambda place: CHUNK_OF["s", place])
-    for place in late[:-1]:
-        combine(place)
-    dk_half[...] = (dk_acc[...] * scaling).astype(BF16)
+    final = [place for place in late if CHUNK_OF["s", place] >= 14]
+    for place in late:
+        if place not in final:
+            combine(place)
+
+    def key_tile(t, carry):
+        def middle():
+            for place in final:
+                combine(place)
+
+        pl.when(t == 1)(middle)
+        here = pl.ds(pl.multiple_of(t * tile, tile), tile)
+        dk = jnp.zeros((tile, 128), F32)
+        dv = jnp.zeros((tile, 128), F32)
+        for c in range(16):
+            dk = dk + jnp.dot(score_buf[c, here], rows_of(c, 0), preferred_element_type=F32)
+            dv = dv + jnp.dot(weight_buf[c, here], rows_of(c, ROWS), preferred_element_type=F32)
+        dk_half[here] = (dk * scaling).astype(BF16)
+        dv_half[here] = dv.astype(BF16)
+        return carry
+
+    lax.fori_loop(0, key_count // tile, key_tile, 0)
     out_k = pltpu.make_async_copy(dk_half, dk_hbm, in_sem.at[0])
     out_k.start()
-    combine(late[-1])
-    dv_half[...] = dv_acc[...].astype(BF16)
     out_v = pltpu.make_async_copy(dv_half, dv_hbm, in_sem.at[1])
     out_v.start()
 
@@ -416,8 +443,8 @@
             pltpu.VMEM((16, 128, ROWS), BF16),
             pltpu.VMEM((16, 128, ROWS), BF16),
             pltpu.VMEM((16, 128, ROWS), BF16),
-            pltpu.VMEM((key_count, 128), F32),
-            pltpu.VMEM((key_count, 128), F32),
+            pltpu.VMEM((16, key_count, 2 * ROWS), BF16),
+            pltpu.VMEM((16, key_count, 2 * ROWS), BF16),
             pltpu.VMEM((key_count, 128), BF16),
             pltpu.VMEM((key_count, 128), BF16),
             pltpu.VMEM((ROWS, 128), BF16),
@@ -430,7 +457,7 @@
             transcendentals=4096 * key_count,
         ),
         compiler_params=pltpu.CompilerParams(
-            collective_id=0, has_side_effects=True, vmem_limit_bytes=40 * 1024 * 1024
+            collective_id=0, has_side_effects=True, vmem_limit_bytes=60 * 1024 * 1024
         ),
     )(
         queries, attn_out, grad_out, log_norms, query_starts,

time: 58.1 us -> 49.6 us (0.85)
  Pallas kernels: 50.2 us -> 44.7 us
  local copies, waits for them, and re-layouts: 6.87 us -> 3.79 us
    pallas_call x1, Pallas kernels: 50.2 us -> 44.7 us  [local(): pl.pallas_call(functools.partial(kernel, scaling), out_shape=(jax.ShapeDt...]
    unnamed x17 -> x5, local copies, waits for them, and re-layouts: 6.87 us -> 3.79 us
where the time goes in v2:
time: 49.6 us; the launch traced here: 49.1 us
  Pallas kernels  44.7 us (90%)
  local copies, waits for them, and re-layouts  3.79 us (8%)
  between operations  0.64 us (1%)
    pallas_call x1, Pallas kernels, local(): pl.pallas_call(functools.partial(kernel, scaling), out_shape=(jax.ShapeDt...  44.7 us
    unnamed x5, local copies, waits for them, and re-layouts  3.79 us

profile of v2, /device:TPU:2, one launch (start us, length us, event | category | flops | bytes accessed | tf_op | source)
XLA Modules:
  0.0 49.1 jit_solution(1922799359189871714)
XLA Ops:
  0.6 44.7 %shard_map.94 = (bf16[2,64,128]{2,1,0:T(8,128)(2,1)}, bf16[1024,128]{1,0:T(8,128)(2,1)}, bf16[1024,128]{1,0:T(8,128)(2,1)}) custom-call(bf16[2,64,128]{2,1,0:T(8,128)(2,1)} %q_hbm.1, bf16[2,64,128]{2,1,0:T(8,128)(2,1)} %o_hbm.1, bf16[2,64,128]{2,1,0:T(8,128)(2,1)} %g_hbm.1, f32[2,64]{1,0:T(2,128)} %n_hbm.1, s32[512]{0:T(512)} %st_hbm.1, ...), custom_call_target="tpu_custom_call" | custom-call | flops 5368709120 | bytes 1048576 | tf_op jit(solution)/shard_map/pallas_call | solution.py:419
  45.3 1.4 %copy.13 = bf16[2,64,128]{2,1,0:T(8,128)(2,1)} copy(bf16[2,64,128]{2,1,0:T(8,128)(2,1)} %get-tuple-element.12) | data formatting | bytes 65536
  46.7 0.0 copy-start
  46.7 1.7 %copy.14 = bf16[1024,1,128]{2,0,1:T(8,128)(2,1)} copy(bf16[1024,1,128]{2,0,1:T(8,128)(2,1)} %bitcast.5) | data formatting | bytes 524288
  48.4 0.0 copy-done
  48.4 0.7 %copy.15 = bf16[1024,1,128]{2,0,1:T(8,128)(2,1)} copy(bf16[1024,1,128]{2,0,1:T(8,128)(2,1)S(1)} %bitcast.4) | data formatting | bytes 524288
Async XLA Ops:
  46.7 1.7 %copy-start = (bf16[1024,128]{1,0:T(8,128)(2,1)S(1)}, bf16[1024,128]{1,0:T(8,128)(2,1)}, u32[]{:S(2)}) copy-start(bf16[1024,128]{1,0:T(8,128)(2,1)} %get-tuple-element.8) | copy-start | bytes 786436

commit v3 on v2

--- a/solution.py
+++ b/solution.py
@@ -16,37 +16,40 @@
 CHUNKS = (
     (("o", (0, 0)), ("s", (0, 0))),
     (("o", (1, 0)), ("o", (3, 0))),
-    (("o", (0, 1)), ("o", (0, 3))),
     (("s", (1, 0)), ("s", (3, 0))),
-    (("o", (2, 0)), ("o", (0, 2))),
-    (("s", (2, 0)), ("s", (0, 2))),
+    (("o", (2, 0)), ("s", (2, 0))),
     (("o", (1, 1)), ("o", (1, 3))),
     (("o", (3, 1)), ("o", (3, 3))),
     (("s", (1, 1)), ("s", (1, 3))),
+    (("s", (3, 1)), ("s", (3, 3))),
     (("o", (1, 2)), ("o", (3, 2))),
-    (("o", (2, 1)), ("o", (2, 3))),
     (("o", (2, 2)), ("s", (2, 2))),
     (("s", (1, 2)), ("s", (3, 2))),
+    (("o", (2, 1)), ("o", (2, 3))),
     (("s", (2, 1)), ("s", (2, 3))),
-    (("s", (3, 1)), ("s", (3, 3))),
+    (("o", (0, 2)), ("s", (0, 2))),
+    (("o", (0, 1)), ("o", (0, 3))),
     (("s", (0, 1)), ("s", (0, 3))),
 )
 ARRIVE = {
     1: ((1, 0), (3, 0)),
-    2: ((2, 0), (0, 1), (0, 3)),
-    4: ((0, 2),),
-    6: ((1, 1), (1, 3)),
-    7: ((3, 1), (3, 3)),
-    9: ((1, 2), (3, 2)),
-    10: ((2, 1), (2, 3), (2, 2)),
+    2: ((2, 0),),
+    4: ((1, 1), (1, 3)),
+    5: ((3, 1), (3, 3)),
+    8: ((1, 2), (3, 2), (2, 2)),
+    10: ((2, 1), (2, 3)),
+    12: ((0, 2),),
+    13: ((0, 1), (0, 3)),
 }
-LAG = 4
+LATE_AT = 2
+LATE = ((0, 2), (0, 1), (0, 3))
+LAG = 3
 SLOT = {name: 2 * c + i for c, pair in enumerate(CHUNKS) for i, name in enumerate(pair)}
 CHUNK_OF = {name: c for c, pair in enumerate(CHUNKS) for name in pair}
 PLACES = [(a, b) for a in range(4) for b in range(4)]
 NUMBER = {place: i for i, place in enumerate(PLACES)}
 MOVES = []
-for _d in [(1, 0), (3, 0), (2, 0), (1, 1), (1, 3), (3, 1), (3, 3), (0, 2), (0, 1), (0, 3)]:
+for _d in [(2, 0), (1, 0), (3, 0), (1, 1), (1, 3), (3, 1), (3, 3), (0, 2), (0, 1), (0, 3)]:
     MOVES += [((0, 0), _d, _d)]
 for _s, _d in [((1, 0), (1, 2)), ((3, 0), (3, 2)), ((2, 0), (2, 2)), ((2, 0), (2, 1)), ((2, 0), (2, 3))]:
     MOVES += [(_s, _d, (0, _d[1]))]
@@ -56,10 +59,10 @@
 def kernel(
     scaling,
     q_hbm, o_hbm, g_hbm, n_hbm, st_hbm, k_hbm, v_hbm,
-    dq_ref, dk_hbm, dv_hbm,
+    dq_ref, dk_half, dv_half,
     q_in, o_in, g_in, n_in, st_in, keys, vals, keys_t, jpos,
     stage, landed, blocks, part, part_half, part_in, total_half, total_in,
-    score_buf, weight_buf, dk_half, dv_half, fin, fin_in,
+    score_buf, weight_buf, fin, fin_in,
     in_sem, az_send, az_recv, mv_send, mv_recv, ps_send, ps_recv, tt_send, tt_recv,
     fz_send, fz_recv,
 ):
@@ -114,7 +117,12 @@
 
     def pass_on(place):
         for n, m in enumerate(MOVES):
-            if m[0] == place:
+            if m[0] == place and (m[1] not in LATE or m[2] == "sib"):
+                move(n).start()
+
+    def pass_late():
+        for n, m in enumerate(MOVES):
+            if m[0] == (0, 0) and m[1] in LATE:
                 move(n).start()
 
     def arrived(kind, place):
@@ -270,6 +278,8 @@
         for place in ARRIVE.get(at_chunk, ()):
             arrived("o", place)
             pass_on(place)
+        if at_chunk == LATE_AT:
+            pass_late()
         for kind, place in CHUNKS[at_chunk]:
             if kind == "s":
                 arrived("s", place)
@@ -342,8 +352,11 @@
             for place in final:
                 combine(place)
 
-        pl.when(t == 1)(middle)
-        here = pl.ds(pl.multiple_of(t * tile, tile), tile)
+        if isinstance(t, int):
+            here = slice(t * tile, (t + 1) * tile)
+        else:
+            pl.when(t == 1)(middle)
+            here = pl.ds(pl.multiple_of(t * tile, tile), tile)
         dk = jnp.zeros((tile, 128), F32)
         dv = jnp.zeros((tile, 128), F32)
         for c in range(16):
@@ -353,11 +366,8 @@
         dv_half[here] = dv.astype(BF16)
         return carry
 
-    lax.fori_loop(0, key_count // tile, key_tile, 0)
-    out_k = pltpu.make_async_copy(dk_half, dk_hbm, in_sem.at[0])
-    out_k.start()
-    out_v = pltpu.make_async_copy(dv_half, dv_hbm, in_sem.at[1])
-    out_v.start()
+    tiles = key_count // tile
+    lax.fori_loop(0, tiles - 1, key_tile, 0)
 
     total = part[SLOT["o", (0, 0)]]
     for place in PLACES[1:]:
@@ -389,6 +399,7 @@
 
     for j in (4, 3, 5, 2, 6, 1, 7):
         send_back(j).start()
+    key_tile(tiles - 1, 0)
     fin_in[k] = fin[pl.ds(pl.multiple_of(16 * k, 16), 16)]
 
     for n in range(len(MOVES)):
@@ -407,24 +418,34 @@
         dq_ref[t] = jnp.concatenate(rows, axis=0).astype(BF16)
     for j in range(1, 8):
         send_back(j).wait_send()
-    out_k.wait()
-    out_v.wait()
+
+
+def write_out(dq_in, dk_in, dv_in, dq_ref, dk_ref, dv_ref, sem):
+    copies = [
+        pltpu.make_async_copy(src, dst, sem.at[i])
+        for i, (src, dst) in enumerate(((dk_in, dk_ref), (dv_in, dv_ref), (dq_in, dq_ref)))
+    ]
+    for copy in copies:
+        copy.start()
+    for copy in copies:
+        copy.wait()
 
 
 def local(queries, attn_out, grad_out, log_norms, query_starts, keys, values):
     scaling = queries.shape[-1] ** (-0.5)
     key_count = keys.shape[0]
     anywhere = pl.BlockSpec(memory_space=pl.ANY)
+    in_hbm = pl.BlockSpec(memory_space=pltpu.HBM)
     sems = [7, 8, 8, len(MOVES), len(MOVES), 16, 16, 16, 16, 8, 8]
     dq, dk, dv = pl.pallas_call(
         functools.partial(kernel, scaling),
         out_shape=(
-            jax.ShapeDtypeStruct((2, 64, 128), BF16),
-            jax.ShapeDtypeStruct((key_count, 128), BF16),
-            jax.ShapeDtypeStruct((key_count, 128), BF16),
+            pltpu.VMEM((2, 64, 128), BF16),
+            pltpu.VMEM((key_count, 128), BF16),
+            pltpu.VMEM((key_count, 128), BF16),
         ),
-        in_specs=[anywhere] * 7,
-        out_specs=(pl.BlockSpec(memory_space=pltpu.VMEM), anywhere, anywhere),
+        in_specs=[in_hbm] * 7,
+        out_specs=(pl.BlockSpec(memory_space=pltpu.VMEM),) * 3,
         scratch_shapes=[
             pltpu.VMEM((2, 64, 128), BF16),
             pltpu.VMEM((2, 64, 128), BF16),
@@ -445,8 +466,6 @@
             pltpu.VMEM((16, 128, ROWS), BF16),
             pltpu.VMEM((16, key_count, 2 * ROWS), BF16),
             pltpu.VMEM((16, key_count, 2 * ROWS), BF16),
-            pltpu.VMEM((key_count, 128), BF16),
-            pltpu.VMEM((key_count, 128), BF16),
             pltpu.VMEM((ROWS, 128), BF16),
             pltpu.VMEM((8, 16, 128), BF16),
             *[pltpu.SemaphoreType.DMA((n,)) for n in sems],
@@ -457,12 +476,24 @@
             transcendentals=4096 * key_count,
         ),
         compiler_params=pltpu.CompilerParams(
-            collective_id=0, has_side_effects=True, vmem_limit_bytes=60 * 1024 * 1024
+            collective_id=0, has_side_effects=True, vmem_limit_bytes=59 * 1024 * 1024
         ),
     )(
         queries, attn_out, grad_out, log_norms, query_starts,
         keys.reshape(key_count, 128), values.reshape(key_count, 128),
     )
+    dq, dk, dv = pl.pallas_call(
+        write_out,
+        out_shape=(
+            jax.ShapeDtypeStruct((2, 64, 128), BF16),
+            jax.ShapeDtypeStruct((key_count, 128), BF16),
+            jax.ShapeDtypeStruct((key_count, 128), BF16),
+        ),
+        in_specs=[pl.BlockSpec(memory_space=pltpu.VMEM)] * 3,
+        out_specs=(anywhere,) * 3,
+        scratch_shapes=[pltpu.SemaphoreType.DMA((3,))],
+        compiler_params=pltpu.CompilerParams(vmem_limit_bytes=1024 * 1024),
+    )(dq, dk, dv)
     return dq, dk[:, None, :], dv[:, None, :]
 
 

time: 49.6 us -> 44 us (0.89)
  local copies, waits for them, and re-layouts: 3.79 us -> 0 us
  Pallas kernels: 44.7 us -> 43.2 us
    unnamed x5 -> x0, local copies, waits for them, and re-layouts: 3.79 us -> none
    pallas_call x1 -> x2, Pallas kernels: 44.7 us -> 43.2 us  [the longest x1 42.4 us: local(): pl.pallas_call(functools.partial(kernel, scaling), out_shape=(pltpu.VMEM(...]
where the time goes in v3:
time: 44 us; the launch traced here: 43.9 us
  Pallas kernels  43.2 us (98%)
  between operations  0.64 us (1%)
    pallas_call x1, Pallas kernels, local(): pl.pallas_call(functools.partial(kernel, scaling), out_shape=(pltpu.VMEM(...  42.4 us

profile of v3, /device:TPU:2, one launch (start us, length us, event | category | flops | bytes accessed | tf_op | source)
XLA Modules:
  0.0 43.9 jit_solution(1383793573519284060)
XLA Ops:
  0.6 42.4 %shard_map.94 = (bf16[2,64,128]{2,1,0:T(8,128)(2,1)S(1)}, bf16[1024,128]{1,0:T(8,128)(2,1)S(1)}, bf16[1024,128]{1,0:T(8,128)(2,1)S(1)}) custom-call(bf16[2,64,128]{2,1,0:T(8,128)(2,1)} %q_hbm.1, bf16[2,64,128]{2,1,0:T(8,128)(2,1)} %o_hbm.1, bf16[2,64,128]{2,1,0:T(8,128)(2,1)} %g_hbm.1, f32[2,64]{1,0:T(2,128)} %n_hbm.1, s32[512]{0:T(512)} %st_hbm.1, ...), custom_call_target="tpu_custom_call" | custom-call | flops 5368709120 | bytes 1048576 | tf_op jit(solution)/shard_map/pallas_call | solution.py:440
  43.0 0.8 %shard_map.95 = (bf16[2,64,128]{2,1,0:T(8,128)(2,1)}, bf16[1024,128]{1,0:T(8,128)(2,1)}, bf16[1024,128]{1,0:T(8,128)(2,1)}) custom-call(bf16[2,64,128]{2,1,0:T(8,128)(2,1)S(1)} %get-tuple-element.9.dq_in, bf16[1024,128]{1,0:T(8,128)(2,1)S(1)} %get-tuple-element.10.dk_in, bf16[1024,128]{1,0:T(8,128)(2,1)S(1)} %get-tuple-element.11.dv_in), custom_call_target="tpu_custom_call" | custom-call | tf_op jit(solution)/shard_map/pallas_call | solution.py:485

commit v4 on v3

--- a/solution.py
+++ b/solution.py
@@ -14,46 +14,35 @@
 ROWS = 128
 BLOCK = 2 * ROWS + 16
 CHUNKS = (
-    (("o", (0, 0)), ("s", (0, 0))),
-    (("o", (1, 0)), ("o", (3, 0))),
-    (("s", (1, 0)), ("s", (3, 0))),
-    (("o", (2, 0)), ("s", (2, 0))),
-    (("o", (1, 1)), ("o", (1, 3))),
-    (("o", (3, 1)), ("o", (3, 3))),
-    (("s", (1, 1)), ("s", (1, 3))),
-    (("s", (3, 1)), ("s", (3, 3))),
-    (("o", (1, 2)), ("o", (3, 2))),
-    (("o", (2, 2)), ("s", (2, 2))),
-    (("s", (1, 2)), ("s", (3, 2))),
-    (("o", (2, 1)), ("o", (2, 3))),
-    (("s", (2, 1)), ("s", (2, 3))),
-    (("o", (0, 2)), ("s", (0, 2))),
-    (("o", (0, 1)), ("o", (0, 3))),
-    (("s", (0, 1)), ("s", (0, 3))),
+    ((1, 0), (3, 0)),
+    ((0, 0), (2, 0)),
+    ((1, 1), (1, 3)),
+    ((1, 2), (3, 2)),
+    ((2, 2), (2, 1)),
+    ((2, 3), (0, 2)),
+    ((3, 1), (3, 3)),
+    ((0, 1), (0, 3)),
 )
+N_CHUNKS = len(CHUNKS)
 ARRIVE = {
-    1: ((1, 0), (3, 0)),
-    2: ((2, 0),),
-    4: ((1, 1), (1, 3)),
-    5: ((3, 1), (3, 3)),
-    8: ((1, 2), (3, 2), (2, 2)),
-    10: ((2, 1), (2, 3)),
-    12: ((0, 2),),
-    13: ((0, 1), (0, 3)),
+    0: ((1, 0), (3, 0)),
+    2: ((1, 1), (1, 3)),
+    3: ((1, 2), (3, 2)),
+    4: ((2, 2), (2, 1)),
+    5: ((2, 3), (0, 2)),
+    6: ((3, 1), (3, 3)),
+    7: ((0, 1), (0, 3)),
 }
+BETWEEN = {0: ((2, 0),)}
 LATE_AT = 2
 LATE = ((0, 2), (0, 1), (0, 3))
-LAG = 3
-SLOT = {name: 2 * c + i for c, pair in enumerate(CHUNKS) for i, name in enumerate(pair)}
-CHUNK_OF = {name: c for c, pair in enumerate(CHUNKS) for name in pair}
+SLOT = {place: 2 * c + i for c, pair in enumerate(CHUNKS) for i, place in enumerate(pair)}
 PLACES = [(a, b) for a in range(4) for b in range(4)]
-NUMBER = {place: i for i, place in enumerate(PLACES)}
 MOVES = []
 for _d in [(2, 0), (1, 0), (3, 0), (1, 1), (1, 3), (3, 1), (3, 3), (0, 2), (0, 1), (0, 3)]:
     MOVES += [((0, 0), _d, _d)]
 for _s, _d in [((1, 0), (1, 2)), ((3, 0), (3, 2)), ((2, 0), (2, 2)), ((2, 0), (2, 1)), ((2, 0), (2, 3))]:
     MOVES += [(_s, _d, (0, _d[1]))]
-MOVES = [(place, place, "sib") for place in PLACES] + MOVES
 
 
 def kernel(
@@ -61,9 +50,9 @@
     q_hbm, o_hbm, g_hbm, n_hbm, st_hbm, k_hbm, v_hbm,
     dq_ref, dk_half, dv_half,
     q_in, o_in, g_in, n_in, st_in, keys, vals, keys_t, jpos,
-    stage, landed, blocks, part, part_half, part_in, total_half, total_in,
-    score_buf, weight_buf, fin, fin_in,
-    in_sem, az_send, az_recv, mv_send, mv_recv, ps_send, ps_recv, tt_send, tt_recv,
+    stage, landed, blocks, part, total_half, total_in,
+    score_buf, weight_buf, other_k, other_v, own_k, own_v, got_k, got_v, fin, fin_in,
+    in_sem, az_send, az_recv, mv_send, mv_recv, xs_send, xs_recv, tt_send, tt_recv,
     fz_send, fz_recv,
 ):
     s, k = lax.axis_index("seq"), lax.axis_index("kvh")
@@ -74,18 +63,16 @@
         return (1 - core) * ((a * 4 + b) * 2) + core * ((b * 4 + a) * 2 + 1)
 
     sibling = s + 1 - 2 * core
-    target = {
-        "sib": sibling,
-    }
-    for a, b in PLACES[1:]:
-        target[a, b] = at((pa + a) % 4, (pb + b) % 4)
+    target = {(a, b): at((pa + a) % 4, (pb + b) % 4) for a, b in PLACES[1:]}
+    key_count = keys.shape[0] // 2
+    mine_at = pl.ds(pl.multiple_of(core * key_count, key_count), key_count)
 
     ins = [
         pltpu.make_async_copy(src, dst, in_sem.at[i])
         for i, (src, dst) in enumerate(
             (
                 (g_hbm, g_in), (o_hbm, o_in), (n_hbm, n_in), (st_hbm, st_in), (q_hbm, q_in),
-                (k_hbm, keys), (v_hbm, vals),
+                (k_hbm, keys.at[mine_at]), (v_hbm, vals.at[mine_at]),
             )
         )
     ]
@@ -105,10 +92,9 @@
 
     def move(n):
         source, dest, way = MOVES[n]
-        kind = "s" if way == "sib" else "o"
-        return pltpu.make_async_remote_copy(
-            src_ref=blocks.at[SLOT["o", source]],
-            dst_ref=blocks.at[SLOT[kind, dest]],
+        return pltpu.make_async_remote_copy(
+            src_ref=blocks.at[SLOT[source]],
+            dst_ref=blocks.at[SLOT[dest]],
             send_sem=mv_send.at[n],
             recv_sem=mv_recv.at[n],
             device_id={"seq": target[way]},
@@ -117,7 +103,7 @@
 
     def pass_on(place):
         for n, m in enumerate(MOVES):
-            if m[0] == place and (m[1] not in LATE or m[2] == "sib"):
+            if m[0] == place and m[1] not in LATE:
                 move(n).start()
 
     def pass_late():
@@ -125,24 +111,30 @@
             if m[0] == (0, 0) and m[1] in LATE:
                 move(n).start()
 
-    def arrived(kind, place):
+    def arrived(place):
         for n, m in enumerate(MOVES):
-            if m[1] == place and (m[2] == "sib") == (kind == "s"):
+            if m[1] == place:
                 move(n).wait_recv()
 
-    def give_part(place):
-        n = NUMBER[place]
-        return pltpu.make_async_remote_copy(
-            src_ref=part_half.at[SLOT["s", place]],
-            dst_ref=part_in.at[n],
-            send_sem=ps_send.at[n],
-            recv_sem=ps_recv.at[n],
+    def to_sibling(n, src, dst):
+        return pltpu.make_async_remote_copy(
+            src_ref=src,
+            dst_ref=dst,
+            send_sem=xs_send.at[n],
+            recv_sem=xs_recv.at[n],
             device_id={"seq": sibling},
             device_id_type=MESH,
         )
 
+    other_at = pl.ds(pl.multiple_of((1 - core) * key_count, key_count), key_count)
+    cached = [to_sibling(n, ref.at[mine_at], ref.at[mine_at]) for n, ref in enumerate((keys, vals))]
+    cached_in = [
+        to_sibling(n, ref.at[other_at], ref.at[other_at]) for n, ref in enumerate((keys, vals))
+    ]
+    halves = [to_sibling(2, other_k, got_k), to_sibling(3, other_v, got_v)]
+
     def give_total(place):
-        n = NUMBER[place]
+        n = SLOT[place]
         a, b = place
         return pltpu.make_async_remote_copy(
             src_ref=total_half.at[n],
@@ -152,16 +144,6 @@
             device_id={"seq": at((pa - a + 4) % 4, (pb - b + 4) % 4)},
             device_id_type=MESH,
         )
-
-    def combine(place):
-        give_part(place).wait_recv()
-        n = NUMBER[place]
-        both = part[SLOT["o", place]] + part_in[n].astype(F32)
-        if place == (0, 0):
-            part[SLOT["o", place]] = both
-        else:
-            total_half[n] = both.astype(BF16)
-            give_total(place).start()
 
     for copy in ins[:5]:
         copy.wait()
@@ -240,16 +222,19 @@
     for j in (4, 3, 5, 2, 6, 1, 7):
         hand_out(j).start()
     landed[k] = stage[k]
-    key_count = keys.shape[0]
     for copy in ins[5:]:
         copy.wait()
+    for copy in cached:
+        copy.start()
+    for copy in cached_in:
+        copy.wait_recv()
     keys_t[...] = keys[...].astype(F32).T.astype(BF16)
-    is_last = jnp.where(s == 31, 1.0, 0.0).astype(F32)
+    is_last = jnp.where(s // 2 == 15, 1.0, 0.0).astype(F32)
     sign = 1.0 - 2.0 * is_last
-    jpos[...] = sign * lax.broadcasted_iota(jnp.int32, (key_count, 128), 0).astype(F32)
+    jpos[...] = sign * lax.broadcasted_iota(jnp.int32, jpos.shape, 0).astype(F32)
     for j in range(1, 8):
         hand_in(j).wait_recv()
-    mine = SLOT["o", (0, 0)]
+    mine = SLOT[0, 0]
     aux = jnp.zeros((16, 128), F32)
     for j in range(8):
         blocks[mine, 16 * j : 16 * (j + 1)] = landed[j, 0:16]
@@ -258,9 +243,9 @@
     blocks[mine, 2 * ROWS : BLOCK] = aux.astype(BF16)
     pass_on((0, 0))
 
-    shift = (s * key_count).astype(F32)
+    shift = ((s // 2) * (2 * key_count)).astype(F32)
     in_block = (lax.broadcasted_iota(jnp.int32, (1, 256), 1) % 128) // 8
-    last_bound = -(512.0 + in_block.astype(F32))
+    last_bound = -(1536.0 + in_block.astype(F32))
     factor = scaling * math.log2(math.e)
     tile = 256
 
@@ -272,26 +257,27 @@
         for i in range(2):
             mine = dq[:, i * ROWS : (i + 1) * ROWS]
             part[2 * c + i] = mine
-            part_half[2 * c + i] = mine.astype(BF16)
+            total_half[2 * c + i] = mine.astype(BF16)
 
     def events(at_chunk):
         for place in ARRIVE.get(at_chunk, ()):
-            arrived("o", place)
+            arrived(place)
             pass_on(place)
         if at_chunk == LATE_AT:
             pass_late()
-        for kind, place in CHUNKS[at_chunk]:
-            if kind == "s":
-                arrived("s", place)
-        for place in PLACES:
-            if CHUNK_OF["s", place] + LAG == at_chunk:
-                combine(place)
+
+    def between(at_chunk):
+        give(at_chunk)
+        for place in BETWEEN.get(at_chunk, ()):
+            arrived(place)
+            pass_on(place)
+        if at_chunk + 0.5 == LATE_AT:
+            pass_late()
 
     def give(at_chunk):
-        if at_chunk:
-            for kind, place in CHUNKS[at_chunk - 1]:
-                if kind == "s":
-                    give_part(place).start()
+        for place in CHUNKS[at_chunk - 1] if at_chunk else ():
+            if place != (0, 0):
+                give_total(place).start()
 
     def by_chunk(c, low, high, do):
         if high - low == 1:
@@ -308,7 +294,7 @@
         lax.cond(c < middle, lower, upper)
 
     def chunk_step(c, carry):
-        by_chunk(c, 0, 16, events)
+        by_chunk(c, 0, N_CHUNKS, events)
 
         before = jnp.maximum(c - 1, 0)
         query_part(before)
@@ -320,7 +306,10 @@
         first = aux[6:7] * 128.0 + aux[7:8] - shift
         bound = jnp.where(is_last > 0.5, last_bound - 16.0 * aux[8:9], first)
         q, g = rows_of(c, 0), rows_of(c, ROWS)
-        for t in range(key_count // tile):
+        steps = 2 * key_count // tile
+        for t in range(steps):
+            if t == steps // 2:
+                by_chunk(c, 0, N_CHUNKS, between)
             here = slice(t * tile, (t + 1) * tile)
             scores = lax.dot_general(keys[here], q, contract_last, preferred_element_type=F32)
             pos = jpos[here]
@@ -330,49 +319,42 @@
             weight_buf[c, here] = weights.astype(BF16)
             score_buf[c, here] = (weights * (grads - delta)).astype(BF16)
 
-        by_chunk(c, 0, 16, give)
         return carry
 
     score_buf[0] = jnp.zeros(score_buf.shape[1:], BF16)
-    lax.fori_loop(0, 16, chunk_step, 0)
-    query_part(15)
-    for kind, place in CHUNKS[15]:
-        if kind == "s":
-            give_part(place).start()
-
-    late = [place for place in PLACES if CHUNK_OF["s", place] + LAG > 15]
-    late = sorted(late, key=lambda place: CHUNK_OF["s", place])
-    final = [place for place in late if CHUNK_OF["s", place] >= 14]
-    for place in late:
-        if place not in final:
-            combine(place)
-
-    def key_tile(t, carry):
-        def middle():
-            for place in final:
-                combine(place)
-
-        if isinstance(t, int):
-            here = slice(t * tile, (t + 1) * tile)
-        else:
-            pl.when(t == 1)(middle)
-            here = pl.ds(pl.multiple_of(t * tile, tile), tile)
+    lax.fori_loop(0, N_CHUNKS, chunk_step, 0)
+    query_part(N_CHUNKS - 1)
+    give(N_CHUNKS)
+
+    def key_tile(first, t, k_ref, v_ref):
+        rows = pl.ds(pl.multiple_of(first * key_count + t * tile, tile), tile)
+        here = pl.ds(pl.multiple_of(t * tile, tile), tile)
         dk = jnp.zeros((tile, 128), F32)
         dv = jnp.zeros((tile, 128), F32)
-        for c in range(16):
-            dk = dk + jnp.dot(score_buf[c, here], rows_of(c, 0), preferred_element_type=F32)
-            dv = dv + jnp.dot(weight_buf[c, here], rows_of(c, ROWS), preferred_element_type=F32)
-        dk_half[here] = (dk * scaling).astype(BF16)
-        dv_half[here] = dv.astype(BF16)
+        for c in range(N_CHUNKS):
+            dk = dk + jnp.dot(score_buf[c, rows], rows_of(c, 0), preferred_element_type=F32)
+            dv = dv + jnp.dot(weight_buf[c, rows], rows_of(c, ROWS), preferred_element_type=F32)
+        k_ref[here] = dk
+        v_ref[here] = dv
+
+    tiles = key_count // tile
+
+    def other_tile(t, carry):
+        key_tile(1 - core, t, other_k, other_v)
         return carry
 
-    tiles = key_count // tile
-    lax.fori_loop(0, tiles - 1, key_tile, 0)
-
-    total = part[SLOT["o", (0, 0)]]
+    def own_tile(t, carry):
+        key_tile(core, t, own_k, own_v)
+        return carry
+
+    lax.fori_loop(0, tiles, other_tile, 0)
+    for copy in halves:
+        copy.start()
+
+    total = part[SLOT[0, 0]]
     for place in PLACES[1:]:
         give_total(place).wait_recv()
-        total = total + total_in[NUMBER[place]].astype(F32)
+        total = total + total_in[SLOT[place]].astype(F32)
     fin[...] = (total.T * scaling).astype(BF16)
 
     def send_back(j):
@@ -399,15 +381,19 @@
 
     for j in (4, 3, 5, 2, 6, 1, 7):
         send_back(j).start()
-    key_tile(tiles - 1, 0)
+    lax.fori_loop(0, tiles, own_tile, 0)
+    for copy in halves:
+        copy.wait_recv()
+    dk_half[...] = ((own_k[...] + got_k[...]) * scaling).astype(BF16)
+    dv_half[...] = (own_v[...] + got_v[...]).astype(BF16)
     fin_in[k] = fin[pl.ds(pl.multiple_of(16 * k, 16), 16)]
 
     for n in range(len(MOVES)):
         move(n).wait_send()
-    for place in PLACES:
-        give_part(place).wait_send()
-        if place != (0, 0):
-            give_total(place).wait_send()
+    for place in PLACES[1:]:
+        give_total(place).wait_send()
+    for copy in cached + halves:
+        copy.wait_send()
     for j in range(1, 8):
         hand_out(j).wait_send()
     for j in range(1, 8):
@@ -436,7 +422,7 @@
     key_count = keys.shape[0]
     anywhere = pl.BlockSpec(memory_space=pl.ANY)
     in_hbm = pl.BlockSpec(memory_space=pltpu.HBM)
-    sems = [7, 8, 8, len(MOVES), len(MOVES), 16, 16, 16, 16, 8, 8]
+    sems = [7, 8, 8, len(MOVES), len(MOVES), 4, 4, 16, 16, 8, 8]
     dq, dk, dv = pl.pallas_call(
         functools.partial(kernel, scaling),
         out_shape=(
@@ -452,20 +438,19 @@
             pltpu.VMEM((2, 64, 128), BF16),
             pltpu.VMEM((2, 64), F32),
             pltpu.SMEM((512,), jnp.int32),
-            pltpu.VMEM((key_count, 128), BF16),
-            pltpu.VMEM((key_count, 128), BF16),
-            pltpu.VMEM((128, key_count), BF16),
-            pltpu.VMEM((key_count, 128), F32),
+            pltpu.VMEM((2 * key_count, 128), BF16),
+            pltpu.VMEM((2 * key_count, 128), BF16),
+            pltpu.VMEM((128, 2 * key_count), BF16),
+            pltpu.VMEM((2 * key_count, 128), F32),
             pltpu.VMEM((8, 48, 128), BF16),
             pltpu.VMEM((8, 48, 128), BF16),
-            pltpu.VMEM((32, BLOCK, 128), BF16),
-            pltpu.VMEM((32, 128, ROWS), F32),
-            pltpu.VMEM((32, 128, ROWS), BF16),
+            pltpu.VMEM((16, BLOCK, 128), BF16),
+            pltpu.VMEM((16, 128, ROWS), F32),
             pltpu.VMEM((16, 128, ROWS), BF16),
             pltpu.VMEM((16, 128, ROWS), BF16),
-            pltpu.VMEM((16, 128, ROWS), BF16),
-            pltpu.VMEM((16, key_count, 2 * ROWS), BF16),
-            pltpu.VMEM((16, key_count, 2 * ROWS), BF16),
+            pltpu.VMEM((N_CHUNKS, 2 * key_count, 2 * ROWS), BF16),
+            pltpu.VMEM((N_CHUNKS, 2 * key_count, 2 * ROWS), BF16),
+            *[pltpu.VMEM((key_count, 128), F32) for _ in range(6)],
             pltpu.VMEM((ROWS, 128), BF16),
             pltpu.VMEM((8, 16, 128), BF16),
             *[pltpu.SemaphoreType.DMA((n,)) for n in sems],

time: 44 us -> 41.3 us (0.939)
  Pallas kernels: 43.2 us -> 40.4 us
    pallas_call x1, Pallas kernels: 42.4 us -> 39.5 us  [local(): pl.pallas_call(functools.partial(kernel, scaling), out_shape=(pltpu.VMEM(...]
where the time goes in v4:
time: 41.3 us; the launch traced here: 41 us
  Pallas kernels  40.4 us (98%)
  between operations  0.64 us (2%)
    pallas_call x1, Pallas kernels, local(): pl.pallas_call(functools.partial(kernel, scaling), out_shape=(pltpu.VMEM(...  39.5 us

profile of v4, /device:TPU:2, one launch (start us, length us, event | category | flops | bytes accessed | tf_op | source)
XLA Modules:
  0.0 41.0 jit_solution(16778600805087827116)
XLA Ops:
  0.6 39.5 %shard_map.94 = (bf16[2,64,128]{2,1,0:T(8,128)(2,1)S(1)}, bf16[1024,128]{1,0:T(8,128)(2,1)S(1)}, bf16[1024,128]{1,0:T(8,128)(2,1)S(1)}) custom-call(bf16[2,64,128]{2,1,0:T(8,128)(2,1)} %q_hbm.1, bf16[2,64,128]{2,1,0:T(8,128)(2,1)} %o_hbm.1, bf16[2,64,128]{2,1,0:T(8,128)(2,1)} %g_hbm.1, f32[2,64]{1,0:T(2,128)} %n_hbm.1, s32[512]{0:T(512)} %st_hbm.1, ...), custom_call_target="tpu_custom_call" | custom-call | flops 5368709120 | bytes 1048576 | tf_op jit(solution)/shard_map/pallas_call | solution.py:426
  40.2 0.8 %shard_map.95 = (bf16[2,64,128]{2,1,0:T(8,128)(2,1)}, bf16[1024,128]{1,0:T(8,128)(2,1)}, bf16[1024,128]{1,0:T(8,128)(2,1)}) custom-call(bf16[2,64,128]{2,1,0:T(8,128)(2,1)S(1)} %get-tuple-element.9.dq_in, bf16[1024,128]{1,0:T(8,128)(2,1)S(1)} %get-tuple-element.10.dk_in, bf16[1024,128]{1,0:T(8,128)(2,1)S(1)} %get-tuple-element.11.dv_in), custom_call_target="tpu_custom_call" | custom-call | tf_op jit(solution)/shard_map/pallas_call | solution.py:470

commit v5 on v4

--- a/solution.py
+++ b/solution.py
@@ -350,6 +350,7 @@
     lax.fori_loop(0, tiles, other_tile, 0)
     for copy in halves:
         copy.start()
+    lax.fori_loop(0, 1, own_tile, 0)
 
     total = part[SLOT[0, 0]]
     for place in PLACES[1:]:
@@ -381,7 +382,7 @@
 
     for j in (4, 3, 5, 2, 6, 1, 7):
         send_back(j).start()
-    lax.fori_loop(0, tiles, own_tile, 0)
+    lax.fori_loop(1, tiles, own_tile, 0)
     for copy in halves:
         copy.wait_recv()
     dk_half[...] = ((own_k[...] + got_k[...]) * scaling).astype(BF16)

time: 41.3 us -> 41.8 us (1.012); the launches traced: 41 us -> 41 us
  no operation moved by 1% of the time
where the time goes in v5:
time: 41.8 us; the launch traced here: 41 us
  Pallas kernels  40.4 us (97%)
  between operations  0.64 us (2%)
    pallas_call x1, Pallas kernels, local(): pl.pallas_call(functools.partial(kernel, scaling), out_shape=(pltpu.VMEM(...  39.5 us

profile of v5, /device:TPU:2, one launch (start us, length us, event | category | flops | bytes accessed | tf_op | source)
XLA Modules:
  0.0 41.0 jit_solution(15799947254004736510)
XLA Ops:
  0.6 39.5 %shard_map.94 = (bf16[2,64,128]{2,1,0:T(8,128)(2,1)S(1)}, bf16[1024,128]{1,0:T(8,128)(2,1)S(1)}, bf16[1024,128]{1,0:T(8,128)(2,1)S(1)}) custom-call(bf16[2,64,128]{2,1,0:T(8,128)(2,1)} %q_hbm.1, bf16[2,64,128]{2,1,0:T(8,128)(2,1)} %o_hbm.1, bf16[2,64,128]{2,1,0:T(8,128)(2,1)} %g_hbm.1, f32[2,64]{1,0:T(2,128)} %n_hbm.1, s32[512]{0:T(512)} %st_hbm.1, ...), custom_call_target="tpu_custom_call" | custom-call | flops 5368709120 | bytes 1048576 | tf_op jit(solution)/shard_map/pallas_call | solution.py:427
  40.2 0.8 %shard_map.95 = (bf16[2,64,128]{2,1,0:T(8,128)(2,1)}, bf16[1024,128]{1,0:T(8,128)(2,1)}, bf16[1024,128]{1,0:T(8,128)(2,1)}) custom-call(bf16[2,64,128]{2,1,0:T(8,128)(2,1)S(1)} %get-tuple-element.9.dq_in, bf16[1024,128]{1,0:T(8,128)(2,1)S(1)} %get-tuple-element.10.dk_in, bf16[1024,128]{1,0:T(8,128)(2,1)S(1)} %get-tuple-element.11.dv_in), custom_call_target="tpu_custom_call" | custom-call | tf_op jit(solution)/shard_map/pallas_call | solution.py:471
